TPU v7x, 128 devices: a whole 4x4x4 slice. The times are simulated.
128 devices in a mesh: dp: 4 (over y_lo, core), fsdp: 32 (over x, z, y_hi).
Axes of the slice: x: 4, y: 4 (y_hi: 2, y_lo: 2; y = y_hi * 2 + y_lo), z: 4, core: 2. Of those that a mesh axis runs over, the one named last changes fastest.
Arguments:
- normed: bfloat16 [65536, 8192], P(('dp', 'fsdp')), may hold values from -24 to 24
- queries: bfloat16 [65536, 4096], P(('dp', 'fsdp')), may hold values from -96 to 96, as said below
- keys: bfloat16 [65536, 512], P(('dp', 'fsdp')), may hold values from -4.5 to 4.5
- value_weight: bfloat16 [8192, 512], P('fsdp'), may hold values from -0.0625 to 0.0625
- iterate: float32 [8192, 512], P('fsdp'), may hold values from -6 to 6
- residual: float32 [8192, 512], P('fsdp'), may hold values from -6 to 6
- direction: float32 [8192, 512], P('fsdp'), may hold values from -6 to 6
- damping: float32 [1], replicated, may hold values from 0.05 to 0.5
Outputs:
- new_iterate: float32 [8192, 512], P('fsdp')
- new_residual: float32 [8192, 512], P('fsdp')
- new_direction: float32 [8192, 512], P('fsdp')
Inputs may be any that keep to these rules, and one draw needn't show every extreme that they name: `queries`: queries are of order one except for a few rows, which may be large multiples of an earlier key of their key-value head.
All inputs are finite; a program needn't handle non-finite values.
Results may differ from a plain program's by a relative error of at most 0.0043.
Values may be sent and summed in bfloat16 or wider, within the bound.
No kernel may reach another device: no remote copies, remote signals or barrier semaphores. Data moves between devices by JAX's collectives and lax.ppermute only.
A program may use at most 192 MiB of HBM per device.

v0:
```python
import math

import jax
import jax.numpy as jnp
from jax import lax
from jax.sharding import PartitionSpec as P

HD = 128


EPSILON = 1e-05


def group_pull(query_rows, key_rows, value_rows, tangent_rows, head_size):
    seq_len = query_rows.shape[0]
    per_group = query_rows.shape[1] // head_size
    queries_split = query_rows.reshape(seq_len, per_group, head_size)
    scores = jnp.einsum(
        "tjd,sd->jts", queries_split, key_rows, preferred_element_type=jnp.float32
    ) / math.sqrt(head_size)
    positions = lax.iota(jnp.int32, seq_len)
    causal = positions[:, None] >= positions[None, :]
    scores = jnp.where(causal, scores, -jnp.inf)
    highest = jnp.max(scores, axis=-1, keepdims=True)
    exps = jnp.exp(scores - highest)
    weights_soft = (exps / jnp.sum(exps, axis=-1, keepdims=True)).astype(jnp.bfloat16)
    outputs = jnp.einsum(
        "jts,sd->tjd", weights_soft, value_rows, preferred_element_type=jnp.float32
    )
    tangents = jnp.einsum(
        "jts,sd->tjd", weights_soft, tangent_rows, preferred_element_type=jnp.float32
    )
    inverse = lax.rsqrt(jnp.mean(outputs * outputs, axis=-1, keepdims=True) + EPSILON)
    normal_out = outputs * inverse

    def jacobian(vector):
        return (
            vector - normal_out * jnp.mean(normal_out * vector, axis=-1, keepdims=True)
        ) * inverse

    wback = jacobian(jacobian(tangents)).astype(jnp.bfloat16)
    return jnp.einsum(
        "jts,tjd->sd", weights_soft, wback, preferred_element_type=jnp.float32
    ).astype(jnp.bfloat16)


def body(normed, queries, keys, value_weight, iterate, residual, direction, damping):
    seq_len = normed.shape[0]
    kv_width = keys.shape[1]
    kv_heads = kv_width // HD
    per_group = queries.shape[1] // kv_width
    dir_half = direction.astype(jnp.bfloat16)
    columns = normed
    projected = jnp.dot(
        columns,
        lax.all_gather(value_weight, "fsdp", axis=0, tiled=True),
        preferred_element_type=jnp.float32,
    )
    tangent = jnp.dot(
        columns,
        lax.all_gather(dir_half, "fsdp", axis=0, tiled=True),
        preferred_element_type=jnp.float32,
    )
    projected = projected.astype(jnp.bfloat16)
    tangent = tangent.astype(jnp.bfloat16)
    pulled_parts = []
    for group_index in range(kv_heads):
        query_cols = queries[:, group_index * per_group * HD : (group_index + 1) * per_group * HD]
        lower = group_index * HD
        pulled_parts.append(
            group_pull(
                query_cols,
                keys[:, lower : lower + HD],
                projected[:, lower : lower + HD],
                tangent[:, lower : lower + HD],
                HD,
            )
        )
    pulled = jnp.concatenate(pulled_parts, axis=1)
    tokens_all = lax.axis_size("dp") * lax.axis_size("fsdp") * seq_len
    columns = normed
    shard_sum = lax.psum_scatter(
        jnp.dot(columns.T, pulled, preferred_element_type=jnp.float32),
        "fsdp",
        scatter_dimension=0,
        tiled=True,
    )
    summed = lax.psum(shard_sum, "dp")
    hessian_dir = summed / tokens_all + damping[0] * direction
    old_sq = lax.psum(jnp.sum(residual * residual), "fsdp")
    curv_sum = lax.psum(jnp.sum(direction * hessian_dir), "fsdp")
    step_size = old_sq / curv_sum
    new_iterate = iterate + step_size * direction
    new_residual = residual - step_size * hessian_dir
    new_sq = lax.psum(jnp.sum(new_residual * new_residual), "fsdp")
    new_direction = new_residual + new_sq / old_sq * direction
    return (new_iterate, new_residual, new_direction)


def solution(mesh):
    return jax.shard_map(
        body,
        mesh=mesh,
        in_specs=(
            P(("dp", "fsdp"), None),
            P(("dp", "fsdp"), None),
            P(("dp", "fsdp"), None),
            P("fsdp", None),
            P("fsdp", None),
            P("fsdp", None),
            P("fsdp", None),
            P(),
        ),
        out_specs=(P("fsdp", None), P("fsdp", None), P("fsdp", None)),
        check_vma=False,
    )
```

profile of v0, /device:TPU:16, one launch (start us, length us, event | category | flops | bytes accessed | tf_op | source)
XLA Modules:
  0.0 863.4 jit_solution(4124391215796967002)
XLA Ops:
  7.9 1.8 convert_element_type.46
  9.8 3.9 fusion.124
  13.7 2.3 copy.97
  16.0 1.4 copy.99
  18.5 7.2 fusion.125
  25.7 7.2 fusion.135
  32.9 7.2 fusion.130
  40.2 7.1 fusion.140
  47.3 7.3 divide_convert_fusion
  54.7 3.5 divide_convert_fusion.2
  58.2 3.5 divide_convert_fusion.1
  62.7 3.3 divide_convert_fusion.3
  66.0 49.0 %all-gather.5.cloned.1.call-done = bf16[8192,512]{1,0:T(8,128)(2,1)} async-done(((bf16[256,512]{1,0:T(8,128)(2,1)}), bf16[8192,512]{1,0:T(8,128)(2,1)}) %all-gather.5.cloned.1.call-update) | async-done | bytes 8388624 | tf_op jit(solution)/shard_map/all_gather | solution.py:56
  115.0 10.4 %convolution_convert_fusion = bf16[512,512]{1,0:T(8,128)(2,1)S(1)} fusion(bf16[512,8192]{1,0:T(8,128)(2,1)} %param.8, bf16[8192,512]{1,0:T(8,128)(2,1)} %all-gather.5.cloned.1.call-done), kind=kOutput, calls=%fused_computation.69 | convolution fusion | flops 4295229440 | bytes 17301504 | tf_op jit(solution)/shard_map/dot_general | solution.py:54
  126.2 94.4 %all-gather.3.cloned.1.call-done = bf16[8192,512]{1,0:T(8,128)(2,1)} async-done(((bf16[256,512]{1,0:T(8,128)(2,1)}), bf16[8192,512]{1,0:T(8,128)(2,1)}) %all-gather.3.cloned.1.call-update) | async-done | bytes 8388624 | tf_op jit(solution)/shard_map/all_gather | solution.py:61
  220.6 10.4 %convolution_convert_fusion.1 = bf16[512,512]{1,0:T(8,128)(2,1)S(1)} fusion(bf16[512,8192]{1,0:T(8,128)(2,1)} %param.8, bf16[8192,512]{1,0:T(8,128)(2,1)} %all-gather.3.cloned.1.call-done), kind=kOutput, calls=%fused_computation.70 | convolution fusion | flops 4295229440 | bytes 17301504 | tf_op jit(solution)/shard_map/dot_general | solution.py:59
  232.4 1.5 fusion.35
  241.1 1.3 fusion.34
  247.8 8.2 convolution_bitcast_fusion
  256.0 360.2 %reduce-scatter.2.cloned.1.call-done = f32[256,512]{0,1:T(8,128)} async-done(((f32[8192,512]{0,1:T(8,128)}), f32[256,512]{0,1:T(8,128)}) %reduce-scatter.2.cloned.1.call-update) | async-done | bytes 524304 | tf_op jit(solution)/shard_map/reduce_scatter | solution.py:82
  618.1 43.0 %all-reduce.3.cloned.1.call-done = f32[256,512]{0,1:T(8,128)} async-done(((f32[256,512]{0,1:T(8,128)}), f32[256,512]{0,1:T(8,128)}) %all-reduce.3.cloned.1.call-update) | async-done | bytes 524304 | tf_op jit(solution)/shard_map/psum | solution.py:88
  661.1 1.9 multiply_reduce_fusion.5
  663.2 90.6 %all-reduce = (f32[]{:T(128)}, f32[]{:T(128)}) all-reduce(f32[]{:T(128)} %multiply_reduce_fusion.6, f32[]{:T(128)} %multiply_reduce_fusion.5), channel_id=1, replica_groups=mesh['dp'=4,'fsdp'=32] {'fsdp'}, use_global_device_ids=true, to_apply=%region_1.2 | all-reduce | flops 2 | bytes 16 | tf_op jit(solution)/shard_map/psum | solution.py:90
  755.8 96.4 %psum.31 = f32[]{:T(128)} all-reduce(f32[]{:T(128)} %get-tuple-element.11), channel_id=1, replica_groups=mesh['dp'=4,'fsdp'=32] {'fsdp'}, use_global_device_ids=true, to_apply=%region_27.28 | all-reduce | flops 1 | bytes 8 | tf_op jit(solution)/shard_map/psum | solution.py:95
  (85 shorter events, 22.8 us)
Async XLA Ops:
  7.2 107.8 %all-gather.5.cloned.1.call-start = ((), (), s32[]{:S(2)}) async-start(), calls=%async_computation.2 | async-start | bytes 8650752 | tf_op jit(solution)/shard_map/all_gather | solution.py:56
  7.9 212.7 %all-gather.3.cloned.1.call-start = ((), (), s32[]{:S(2)}) async-start(), calls=%async_computation.1 | async-start | bytes 8650752 | tf_op jit(solution)/shard_map/all_gather | solution.py:61
  9.7 606.5 %reduce-scatter.2.cloned.1.call-start = ((), (), s32[]{:S(2)}) async-start(), calls=%async_computation.3 | async-start | bytes 17301504 | tf_op jit(solution)/shard_map/reduce_scatter | solution.py:82
  25.7 7.2 copy-start.10
  32.9 7.2 copy-start.9
  47.3 7.3 copy-start.5
  47.3 10.8 %slice-start.2 = ((s8[8388608]{0:T(1024)(128)(4,1)}), s8[4194304]{0:T(1024)(128)(4,1)S(1)}, s32[]{:S(2)}) async-start(s8[8388608]{0:T(1024)(128)(4,1)} %bitcast.284), calls=%async_computation.7 | async-start | bytes 8388608
  54.7 3.5 slice-start.3
  54.7 6.9 slice-start.4
  58.1 4.6 slice-start.5
  115.0 10.4 %copy-start.3 = (bf16[8,512,512]{1,2,0:T(8,128)(2,1)S(1)}, bf16[8,512,512]{1,2,0:T(8,128)(2,1)}, u32[]{:S(2)}) copy-start(bf16[8,512,512]{1,2,0:T(8,128)(2,1)} %divide_convert_fusion) | copy-start | bytes 12582916
  220.6 10.4 %copy-start.4 = (bf16[8,512,512]{1,2,0:T(8,128)(2,1)S(1)}, bf16[8,512,512]{1,2,0:T(8,128)(2,1)}, u32[]{:S(2)}) copy-start(bf16[8,512,512]{1,2,0:T(8,128)(2,1)} %divide_convert_fusion) | copy-start | bytes 12582916
  232.4 2.2 copy-start.2
  236.8 2.2 copy-start.1
  241.1 2.2 copy-start
  244.1 2.8 slice-start
  244.9 2.9 slice-start.1
  255.9 360.3 %copy-start.6 = (f32[256,512]{1,0:T(8,128)S(1)}, f32[256,512]{1,0:T(8,128)}, u32[]{:S(2)}) copy-start(f32[256,512]{1,0:T(8,128)} %param.14) | copy-start | bytes 1572868
  255.9 361.2 %copy-start.7 = (f32[256,512]{1,0:T(8,128)S(1)}, f32[256,512]{1,0:T(8,128)}, u32[]{:S(2)}) copy-start(f32[256,512]{1,0:T(8,128)} %param.13) | copy-start | bytes 1572868
  256.0 405.1 %all-reduce.3.cloned.1.call-start = ((), (), s32[]{:S(2)}) async-start(), calls=%async_computation.4 | async-start | bytes 1048576 | tf_op jit(solution)/shard_map/psum | solution.py:88
  616.2 46.7 %copy-start.11 = (f32[256,512]{1,0:T(8,128)S(1)}, f32[256,512]{1,0:T(8,128)}, u32[]{:S(2)}) copy-start(f32[256,512]{1,0:T(8,128)} %param.12) | copy-start | bytes 1572868
  661.1 94.0 %copy-start.8 = (f32[256,512]{0,1:T(8,128)S(1)}, f32[256,512]{0,1:T(8,128)}, u32[]{:S(2)}) copy-start(f32[256,512]{0,1:T(8,128)} %all-reduce.3.cloned.1.call-done) | copy-start | bytes 1572868
Sparse Core Ops, SparseCore 0:
  11.0 103.9 all-gather.4
  118.6 101.9 all-gather.2
  256.1 360.0 reduce-scatter.1
  618.6 42.4 all-reduce.2
where the time goes:
time: 874 us; the launch traced here: 863 us
  waiting for transfers between devices  547 us (63%)
  blocking collectives  187 us (21%)
  matrix products  69.2 us (8%)
  other arithmetic  25.3 us (3%)
  between operations  17.7 us (2%)
  local copies, waits for them, and re-layouts  16.7 us (2%)
    reduce_scatter x1, waiting for transfers between devices, body(): lax.psum_scatter(jnp.dot(columns.T, pulled, preferred_element_type=jnp.fl...  360 us
    psum x1, blocking collectives, body(): new_sq = lax.psum(jnp.sum(new_residual * new_residual), 'fsdp')  96.4 us
    all_gather x1, waiting for transfers between devices, body(): lax.all_gather(dir_half, 'fsdp', axis=0, tiled=True)  94.4 us
    psum x1, blocking collectives, body(): old_sq = lax.psum(jnp.sum(residual * residual), 'fsdp')  90.6 us
    all_gather x1, waiting for transfers between devices, body(): lax.all_gather(value_weight, 'fsdp', axis=0, tiled=True)  49 us
    psum x1, waiting for transfers between devices, body(): summed = lax.psum(shard_sum, 'dp')  43 us
    sub x4, matrix products, group_pull(): exps = jnp.exp(scores - highest)  28.8 us
    convert_element_type x4, other arithmetic, group_pull(): (exps / jnp.sum(exps, axis=-1, keepdims=True)).astype(jnp.bfloat16)  17.5 us
  transfers between devices with their start and end apart: 4, of which 4 were waited for; matrix products, arithmetic and copies ran while one was open for 8% of the time, Pallas kernels for 0%

commit v1 on v0

v1 whole, which is shorter than its diff:
```python
import math

import jax
import jax.numpy as jnp
from jax import lax
from jax.experimental import pallas as pl
from jax.experimental.pallas import tpu as pltpu
from jax.sharding import Mesh, PartitionSpec as P

HD = 128
EPSILON = 1e-05
BF = jnp.bfloat16
F32 = jnp.float32
LEN = 512
HALF = 256
WIDE = 256
PER = 8
VMEM = 56 * 1024 * 1024
NT = (((1,), (1,)), ((), ()))
Y_SWAP = [(0, 3), (3, 0), (2, 1), (1, 2)]


def _params(n):
    return pltpu.CompilerParams(
        dimension_semantics=("arbitrary",) * n, vmem_limit_bytes=VMEM
    )


Q_STEP = 4


def _probs_kernel(off, q_ref, k_ref, o_ref):
    del off
    factor = math.log2(math.e) / math.sqrt(HD)
    rows = lax.broadcasted_iota(jnp.int32, (HALF, HALF), 0)
    cols = lax.broadcasted_iota(jnp.int32, (HALF, HALF), 1)
    seen = rows <= cols
    for j in range(Q_STEP):
        q = q_ref[:, j * HD : (j + 1) * HD]
        diag = lax.dot_general(k_ref[:HALF], q[:HALF], NT, preferred_element_type=F32)
        diag = jnp.where(seen, diag, -jnp.inf)
        top = jnp.max(diag, axis=0, keepdims=True)
        e = jnp.exp2((diag - top) * factor)
        o_ref[j, :HALF] = (e * (1.0 / jnp.sum(e, axis=0, keepdims=True))).astype(BF)
        low = lax.dot_general(k_ref[:HALF], q[HALF:], NT, preferred_element_type=F32)
        diag = lax.dot_general(k_ref[HALF:], q[HALF:], NT, preferred_element_type=F32)
        diag = jnp.where(seen, diag, -jnp.inf)
        top = jnp.maximum(
            jnp.max(low, axis=0, keepdims=True), jnp.max(diag, axis=0, keepdims=True)
        )
        e = jnp.exp2((low - top) * factor)
        f = jnp.exp2((diag - top) * factor)
        inv = 1.0 / (
            jnp.sum(e, axis=0, keepdims=True) + jnp.sum(f, axis=0, keepdims=True)
        )
        o_ref[j, HALF : 2 * HALF] = (e * inv).astype(BF)
        o_ref[j, 2 * HALF :] = (f * inv).astype(BF)


def probs_of(offset, queries, keys):
    heads = 2 * PER
    steps = heads // Q_STEP
    per = steps // 2
    return pl.pallas_call(
        _probs_kernel,
        grid_spec=pltpu.PrefetchScalarGridSpec(
            num_scalar_prefetch=1,
            grid=(steps,),
            in_specs=[
                pl.BlockSpec((LEN, Q_STEP * HD), lambda i, o: (0, o[0] * steps + i)),
                pl.BlockSpec((LEN, HD), lambda i, o: (0, o[0] * 2 + i // per)),
            ],
            out_specs=pl.BlockSpec((Q_STEP, 3 * HALF, HALF), lambda i, o: (i, 0, 0)),
        ),
        out_shape=jax.ShapeDtypeStruct((heads, 3 * HALF, HALF), BF),
        compiler_params=_params(1),
        cost_estimate=pl.CostEstimate(
            flops=heads * 3 * HALF * HALF * HD * 2,
            bytes_accessed=heads * 3 * HALF * HALF * 2 + LEN * heads * HD * 2,
            transcendentals=heads * 3 * HALF * HALF,
        ),
    )(offset, queries, keys)


P_ROWS = 256


def _project_kernel(n_v, where, xa_ref, xb_ref, *refs):
    pieces, (o_ref,) = refs[:-1], refs[-1:]
    i = pl.program_id(0)

    def go(x_ref):
        at = 0
        for half, group in enumerate((pieces[:n_v], pieces[n_v:])):
            total = jnp.zeros((P_ROWS, WIDE), F32)
            for piece in group:
                for r in range(piece.shape[0] // 256):
                    c = pl.multiple_of(where[at] * 256, 256)
                    total += jnp.dot(
                        x_ref[:, pl.ds(c, 256)],
                        piece[r * 256 : (r + 1) * 256],
                        preferred_element_type=F32,
                    )
                    at += 1
            o_ref[half * WIDE : (half + 1) * WIDE] = total.T.astype(BF)

    steps = LEN // P_ROWS

    @pl.when(i < steps)
    def _():
        go(xa_ref)

    @pl.when(i >= steps)
    def _():
        go(xb_ref)


def project(where, xa, xb, v_pieces, t_pieces):
    steps = LEN // P_ROWS
    pieces = [*v_pieces, *t_pieces]
    depth = xa.shape[1]
    whole = [pl.BlockSpec(p.shape, lambda i, w: (0, 0)) for p in pieces]

    def kernel(*refs):
        _project_kernel(len(v_pieces), *refs)

    return pl.pallas_call(
        kernel,
        grid_spec=pltpu.PrefetchScalarGridSpec(
            num_scalar_prefetch=1,
            grid=(2 * steps,),
            in_specs=[
                pl.BlockSpec((P_ROWS, depth), lambda i, w: (jnp.minimum(i, steps - 1), 0)),
                pl.BlockSpec((P_ROWS, depth), lambda i, w: (jnp.maximum(i - steps, 0), 0)),
                *whole,
            ],
            out_specs=pl.BlockSpec((2 * WIDE, P_ROWS), lambda i, w: (0, i)),
        ),
        out_shape=jax.ShapeDtypeStruct((2 * WIDE, 2 * LEN), BF),
        compiler_params=_params(1),
        cost_estimate=pl.CostEstimate(
            flops=2 * LEN * depth * 2 * WIDE * 2,
            bytes_accessed=(2 * LEN * depth + depth * 2 * WIDE) * 2,
            transcendentals=0,
        ),
    )(where, xa, xb, *pieces)


H_STEP = 2


def _pull_kernel(p_ref, v_ref, t_ref, o_ref, acc):
    h = pl.program_id(1)

    @pl.when(h == 0)
    def _():
        acc[...] = jnp.zeros_like(acc)

    both = jnp.concatenate([v_ref[...], t_ref[...]], axis=0)

    def back(o):
        out, tan = o[:HD], o[HD:]
        square = jnp.sum(out * out, axis=0, keepdims=True) * (1.0 / HD)
        cross = jnp.sum(out * tan, axis=0, keepdims=True) * (1.0 / HD)
        inv2 = 1.0 / (square + EPSILON)
        pull = inv2 * cross * (1.0 + EPSILON * inv2)
        return (inv2 * (tan - out * pull)).astype(BF)

    for j in range(H_STEP):
        p0, p1 = p_ref[j, :HALF], p_ref[j, HALF:]
        w0 = back(jnp.dot(both[:, :HALF], p0, preferred_element_type=F32))
        w1 = back(jnp.dot(both, p1, preferred_element_type=F32))
        acc[:HALF] += lax.dot_general(p0, w0, NT, preferred_element_type=F32)
        acc[...] += lax.dot_general(p1, w1, NT, preferred_element_type=F32)

    @pl.when(h == PER // H_STEP - 1)
    def _():
        o_ref[...] = acc[...].T.astype(BF)


def pull_back(probs, projected, seq):
    steps = PER // H_STEP
    return pl.pallas_call(
        _pull_kernel,
        grid=(2, steps),
        in_specs=[
            pl.BlockSpec((H_STEP, 3 * HALF, HALF), lambda g, h: (g * steps + h, 0, 0)),
            pl.BlockSpec((HD, LEN), lambda g, h: (g, seq)),
            pl.BlockSpec((HD, LEN), lambda g, h: (2 + g, seq)),
        ],
        out_specs=pl.BlockSpec((HD, LEN), lambda g, h: (g, 0)),
        out_shape=jax.ShapeDtypeStruct((WIDE, LEN), BF),
        scratch_shapes=[pltpu.VMEM((LEN, HD), F32)],
        compiler_params=_params(2),
    )(probs, projected, projected)


G_COLS = 512
OWN = 128


def _ggn_kernel(pa_ref, pb_ref, xa_ref, xb_ref, o_ref):
    total = jnp.dot(pa_ref[...], xa_ref[...], preferred_element_type=F32)
    total += jnp.dot(pb_ref[...], xb_ref[...], preferred_element_type=F32)
    for j in range(G_COLS // OWN):
        o_ref[j] = total[:, j * OWN : (j + 1) * OWN].astype(BF)


def curvature(pa, pb, xa, xb):
    depth = xa.shape[1]
    return pl.pallas_call(
        _ggn_kernel,
        grid=(depth // G_COLS,),
        in_specs=[
            pl.BlockSpec((WIDE, LEN), lambda i: (0, 0)),
            pl.BlockSpec((WIDE, LEN), lambda i: (0, 0)),
            pl.BlockSpec((LEN, G_COLS), lambda i: (0, i)),
            pl.BlockSpec((LEN, G_COLS), lambda i: (0, i)),
        ],
        out_specs=pl.BlockSpec((G_COLS // OWN, WIDE, OWN), lambda i: (i, 0, 0)),
        out_shape=jax.ShapeDtypeStruct((depth // OWN, WIDE, OWN), BF),
        compiler_params=_params(1),
    )(pa, pb, xa, xb)


def hop(x, axis, by):
    return lax.ppermute(x, axis, [(i, (i + by) % 4) for i in range(4)])


def moved(places, axis, by):
    at = "xz".index(axis)
    return [tuple((v + by) % 4 if i == at else v for i, v in enumerate(p)) for p in places]


def ring(x, places, axis):
    half = x.shape[0] // 2
    cut = len(places) // 2
    before, after = hop(x, axis, 1), hop(x, axis, 3)
    far_a = hop(before[:half], axis, 1)
    far_b = hop(after[half:], axis, 3)
    arrays = [x, before, after, far_a, far_b]
    order = [
        places,
        moved(places, axis, -1),
        moved(places, axis, 1),
        moved(places[:cut], axis, 2),
        moved(places[cut:], axis, 2),
    ]
    return arrays, order


def gather_rows(value, tangent):
    rows = value.shape[0]
    joined = jnp.concatenate([value, tangent], axis=0)
    swapped = lax.ppermute(joined, ("yl", "yh"), Y_SWAP)
    value = jnp.concatenate([value, swapped[:rows]], axis=0)
    tangent = jnp.concatenate([tangent, swapped[rows:]], axis=0)
    places = [(0, 0, 0), (0, 0, 1)]
    result = []
    first = [ring(value, places, "x"), ring(tangent, places, "z")]
    for (arrays, order), axis in zip(first, "zx"):
        whole = jnp.concatenate(arrays, axis=0)
        arrays, order = ring(whole, sum(order, []), axis)
        result.append((arrays, sum(order, [])))
    x, z, yh = (lax.axis_index(a) for a in ("x", "z", "yh"))
    where = [
        ((x + p[0]) % 4) * 8 + ((z + p[1]) % 4) * 2 + (yh + p[2]) % 2
        for _, order in result
        for p in order
    ]
    return result[0][0], result[1][0], jnp.stack(where).astype(jnp.int32)


CHIPS = ("x", "z", "yh", "yl")


def body(normed, queries, keys, value_weight, iterate, residual, direction, damping):
    core, yl = lax.axis_index("c"), lax.axis_index("yl")
    other = 1 - core
    swap = [(0, 1), (1, 0)]
    heads = 2 * PER * HD

    def cols(a, which, width):
        return lax.dynamic_slice_in_dim(a, which * width, width, 1)

    value = cols(value_weight, core, WIDE)
    tangent = cols(direction, core, WIDE).astype(BF)
    v_pieces, t_pieces, where = gather_rows(value, tangent)
    queries_b = lax.ppermute(cols(queries, other, heads), "c", swap)
    keys_b = lax.ppermute(cols(keys, other, WIDE), "c", swap)
    normed_b = lax.ppermute(normed, "c", swap)
    probs_a = probs_of(core[None].astype(jnp.int32), queries, keys)
    probs_b = probs_of(jnp.zeros((1,), jnp.int32), queries_b, keys_b)
    projected = project(where, normed, normed_b, v_pieces, t_pieces)
    pulled_a = pull_back(probs_a, projected, 0)
    pulled_b = pull_back(probs_b, projected, 1)
    parts = curvature(pulled_a, pulled_b, normed, normed_b)
    parts = lax.all_to_all(parts, CHIPS, 0, 0, tiled=True)
    tokens_all = lax.axis_size(("c",) + CHIPS) * normed.shape[0]
    summed = jnp.sum(parts.astype(F32), axis=0).T

    def piece(a):
        return lax.dynamic_slice(a, (yl * OWN, core * WIDE), (OWN, WIDE))

    d, r = piece(direction), piece(residual)
    h = summed / tokens_all + damping[0] * d
    sums = jnp.stack([jnp.sum(r * r), jnp.sum(d * h), jnp.sum(r * h), jnp.sum(h * h)])
    everyone = ("c",) + CHIPS
    n = lax.axis_size(everyone)
    row = jnp.zeros((128,), F32).at[:4].set(sums)
    rows = jnp.broadcast_to(row[None], (n, 128))
    rows = lax.all_to_all(rows, everyone, 0, 0, tiled=True)
    total = jnp.sum(rows, axis=0)
    h_c = lax.ppermute(h, "c", swap)
    h_y = lax.ppermute(h, "yl", swap)
    h_yc = lax.ppermute(h, ("yl", "c"), [(i, 3 - i) for i in range(4)])

    def in_order(flag, a, b, axis):
        return jnp.where(
            flag == 0, jnp.concatenate([a, b], axis), jnp.concatenate([b, a], axis)
        )

    hdir = in_order(yl, in_order(core, h, h_c, 1), in_order(core, h_y, h_yc, 1), 0)
    rr, ph, rh, hh = total[0], total[1], total[2], total[3]
    step = rr / ph
    nn = rr - 2.0 * step * rh + step * step * hh
    new_iterate = iterate + step * direction
    new_residual = residual - step * hdir
    new_direction = new_residual + nn / rr * direction
    return (new_iterate, new_residual, new_direction)


def solution(mesh):
    fine = Mesh(
        mesh.devices.reshape(2, 2, 4, 4, 2), ("yl", "c", "x", "z", "yh")
    )
    tokens = P(("yl", "c", "x", "z", "yh"), None)
    rows = P(("x", "z", "yh"), None)
    return jax.shard_map(
        body,
        mesh=fine,
        in_specs=(tokens, tokens, tokens, rows, rows, rows, rows, P()),
        out_specs=(rows, rows, rows),
        check_vma=False,
    )
```

time: 874 us -> 270 us (0.31)
  waiting for transfers between devices: 547 us -> 113 us
  blocking collectives: 187 us -> 0 us
  matrix products: 69.2 us -> 0 us
  Pallas kernels: 0 us -> 67.7 us
  starting transfers between devices: 0.16 us -> 51.7 us
  other arithmetic: 25.3 us -> 6.36 us
  between operations: 17.7 us -> 5.26 us
    reduce_scatter x1 -> x0, waiting for transfers between devices: 360 us -> none  [body(): lax.psum_scatter(jnp.dot(columns.T, pulled, preferred_element_type=jnp.fl...]
    psum x2 -> x0, blocking collectives: 187 us -> none  [the longest x1 96.4 us: body(): new_sq = lax.psum(jnp.sum(new_residual * new_residual), 'fsdp')]
    all_gather x2 -> x0, waiting for transfers between devices: 143 us -> none  [the longest x1 94.4 us: body(): lax.all_gather(dir_half, 'fsdp', axis=0, tiled=True)]
    pallas_call x0 -> x6, Pallas kernels: none -> 67.7 us  [the longest x2 20.2 us: pull_back(): pl.pallas_call(_pull_kernel, grid=(2, steps), in_specs=[pl.BlockSpec((H_S...]
    ppermute x0 -> x23, waiting for transfers between devices: none -> 56.9 us  [the longest x16 48.6 us: hop(): return lax.ppermute(x, axis, [(i, (i + by) % 4) for i in range(4)])]
    all_to_all x0 -> x2, waiting for transfers between devices: none -> 55.8 us  [the longest x1 50.1 us: body(): parts = lax.all_to_all(parts, CHIPS, 0, 0, tiled=True)]
    psum x1 -> x0, waiting for transfers between devices: 43 us -> none  [body(): summed = lax.psum(shard_sum, 'dp')]
    dot_general x15 -> x0, matrix products: 40.5 us -> none  [the longest x1 10.4 us: body(): jnp.dot(columns, lax.all_gather(dir_half, 'fsdp', axis=0, tiled=True), pr...]
  transfers between devices with their start and end apart: 4 -> 25, of which waited for: 4 -> 9; matrix products, arithmetic and copies ran while one was open for 8% -> 7% of each run, Pallas kernels for 0% -> 5%
where the time goes in v1:
time: 270 us; the launch traced here: 266 us
  waiting for transfers between devices  113 us (42%)
  Pallas kernels  67.7 us (25%)
  starting transfers between devices  51.7 us (19%)
  local copies, waits for them, and re-layouts  22.7 us (8%)
  other arithmetic  6.36 us (2%)
  between operations  5.26 us (2%)
    all_to_all x1, waiting for transfers between devices, body(): parts = lax.all_to_all(parts, CHIPS, 0, 0, tiled=True)  50.1 us
    ppermute x16, waiting for transfers between devices, hop(): return lax.ppermute(x, axis, [(i, (i + by) % 4) for i in range(4)])  48.6 us
    ppermute x16, starting transfers between devices, hop(): return lax.ppermute(x, axis, [(i, (i + by) % 4) for i in range(4)])  25.9 us
    pallas_call x2, Pallas kernels, pull_back(): pl.pallas_call(_pull_kernel, grid=(2, steps), in_specs=[pl.BlockSpec((H_S...  20.2 us
    pallas_call x1, Pallas kernels, project(): pl.pallas_call(kernel, grid_spec=pltpu.PrefetchScalarGridSpec(num_scalar_...  17.4 us
    pallas_call x1, Pallas kernels, curvature(): pl.pallas_call(_ggn_kernel, grid=(depth // G_COLS,), in_specs=[pl.BlockSp...  15.9 us
    all_to_all x1, starting transfers between devices, body(): rows = lax.all_to_all(rows, everyone, 0, 0, tiled=True)  15.8 us
    pallas_call x2, Pallas kernels, probs_of(): pl.pallas_call(_probs_kernel, grid_spec=pltpu.PrefetchScalarGridSpec(num_...  14.2 us
  transfers between devices with their start and end apart: 25, of which 9 were waited for; matrix products, arithmetic and copies ran while one was open for 7% of the time, Pallas kernels for 5%

profile of v1, /device:TPU:16, one launch (start us, length us, event | category | flops | bytes accessed | tf_op | source)
XLA Modules:
  0.0 266.4 jit_solution(14056053182644853705)
XLA Ops:
  3.1 8.2 %collective-permute-done.1 = bf16[512,256]{1,0:T(8,128)(2,1)S(1)} collective-permute-done((bf16[512,256]{1,0:T(8,128)(2,1)S(1)}, bf16[512,256]{1,0:T(8,128)(2,1)S(1)}, u32[]{:S(2)}, u32[]{:S(2)}) %collective-permute-start.1) | collective-permute-done | bytes 262176 | tf_op jit(solution)/shard_map/ppermute | solution.py:255
  12.0 2.0 collective-permute-start.10
  14.0 2.2 collective-permute-start.11
  16.2 6.1 %collective-permute-done.10 = bf16[512,256]{1,0:T(8,128)(2,1)S(1)} collective-permute-done((bf16[512,256]{1,0:T(8,128)(2,1)S(1)}, bf16[512,256]{1,0:T(8,128)(2,1)S(1)}, u32[]{:S(2)}, u32[]{:S(2)}) %collective-permute-start.10) | collective-permute-done | bytes 262176 | tf_op jit(solution)/shard_map/ppermute | solution.py:227
  22.4 3.3 %collective-permute-start.13 = (bf16[256,256]{1,0:T(8,128)(2,1)S(1)}, bf16[256,256]{1,0:T(8,128)(2,1)S(1)}, u32[]{:S(2)}, u32[]{:S(2)}) collective-permute-start(bf16[256,256]{1,0:T(8,128)(2,1)S(1)} %slice.74), channel_id=1, source_target_pairs={{0,6},{2,0},{4,2},{6,4},{1,7},{3,1},{5,3},{7,5},{8,14},{10,8},{12,... | collective-permute-start | bytes 393224 | tf_op jit(solution)/shard_map/ppermute | solution.py:227
  31.4 3.2 %constant_dynamic-slice_fusion.1 = bf16[512,2048]{1,0:T(8,128)(2,1)} fusion(bf16[512,4096]{1,0:T(8,128)(2,1)} %q_ref.1, s32[]{:T(128)S(6)} %select_n.455), kind=kLoop, calls=%fused_computation.30 | loop fusion | bytes 4194308 | tf_op jit(solution)/shard_map/dynamic_slice | solution.py:284
  37.9 22.0 %collective-permute-done.2 = bf16[512,256]{1,0:T(8,128)(2,1)S(1)} collective-permute-done((bf16[512,256]{1,0:T(8,128)(2,1)S(1)}, bf16[512,256]{1,0:T(8,128)(2,1)S(1)}, u32[]{:S(2)}, u32[]{:S(2)}) %collective-permute-start.2) | collective-permute-done | bytes 262176 | tf_op jit(solution)/shard_map/ppermute | solution.py:227
  60.5 2.9 %collective-permute-start.5 = (bf16[256,256]{1,0:T(8,128)(2,1)S(1)}, bf16[256,256]{1,0:T(8,128)(2,1)S(1)}, u32[]{:S(2)}, u32[]{:S(2)}) collective-permute-start(bf16[256,256]{1,0:T(8,128)(2,1)S(1)} %slice.69), channel_id=1, source_target_pairs={{0,24},{8,0},{16,8},{24,16},{1,25},{9,1},{17,9},{25,17},{2,26},{10... | collective-permute-start | bytes 393224 | tf_op jit(solution)/shard_map/ppermute | solution.py:227
  64.1 2.1 collective-permute-done.4
  68.7 3.2 %collective-permute-start.7 = (bf16[2048,256]{1,0:T(8,128)(2,1)}, bf16[2048,256]{1,0:T(8,128)(2,1)}, u32[]{:S(2)}, u32[]{:S(2)}) collective-permute-start(bf16[2048,256]{1,0:T(8,128)(2,1)} %constant_dynamic-update-slice_fusion.refs_3_), channel_id=1, source_target_pairs={{0,6},{2,0},{4,2},{6,4},{1,7},{3,1},{5,3},{7,5},{8,14},{10,8},{12,... | collective-permute-start | bytes 3145736 | tf_op jit(solution)/shard_map/ppermute | solution.py:227
  72.0 16.1 %collective-permute-done.15.refs_10_ = bf16[2048,256]{1,0:T(8,128)(2,1)} collective-permute-done((bf16[2048,256]{1,0:T(8,128)(2,1)}, bf16[2048,256]{1,0:T(8,128)(2,1)}, u32[]{:S(2)}, u32[]{:S(2)}) %collective-permute-start.15) | collective-permute-done | bytes 1048608 | tf_op jit(solution)/shard_map/ppermute | solution.py:227
  98.1 3.2 %collective-permute-start.9 = (bf16[1024,256]{1,0:T(8,128)(2,1)}, bf16[1024,256]{1,0:T(8,128)(2,1)}, u32[]{:S(2)}, u32[]{:S(2)}) collective-permute-start(bf16[1024,256]{1,0:T(8,128)(2,1)} %slice.71), channel_id=1, source_target_pairs={{0,6},{2,0},{4,2},{6,4},{1,7},{3,1},{5,3},{7,5},{8,14},{10,8},{12,... | collective-permute-start | bytes 1572872 | tf_op jit(solution)/shard_map/ppermute | solution.py:227
  102.0 7.1 %shard_map.103.p_ref = bf16[16,768,256]{2,1,0:T(8,128)(2,1)} custom-call(s32[1]{0:T(128)} %bitcast.1.off, bf16[512,4096]{1,0:T(8,128)(2,1)} %q_ref.1, bf16[512,512]{1,0:T(8,128)(2,1)} %k_ref.1), custom_call_target="tpu_custom_call" | custom-call | flops 805306368 | bytes 8388608 | tf_op jit(solution)/shard_map/pallas_call | solution.py:64
  109.1 7.1 %shard_map.106.p_ref = bf16[16,768,256]{2,1,0:T(8,128)(2,1)} custom-call(s32[1]{0:T(128)} %constant.484.clone.1.off, bf16[512,2048]{1,0:T(8,128)(2,1)} %copy-done, bf16[512,256]{1,0:T(8,128)(2,1)} %copy-done.5), custom_call_target="tpu_custom_call" | custom-call | flops 805306368 | bytes 8388608 | tf_op jit(solution)/shard_map/pallas_call | solution.py:64
  116.3 17.4 %shard_map.104.v_ref.t_ref = bf16[512,1024]{1,0:T(8,128)(2,1)} custom-call(s32[64]{0:T(128)} %stack.179.refs_0_, bf16[512,8192]{1,0:T(8,128)(2,1)} %xa_ref.1, bf16[512,8192]{1,0:T(8,128)(2,1)} %collective-permute-done.refs_2_.xb_ref, bf16[2048,256]{1,0:T(8,128)(2,1)} %constant_dynamic-update-slice_fusion.refs_3_, ...), custom_call_target="tpu_custom_call" | custom-call | flops 8589934592 | bytes 25165824 | tf_op jit(solution)/shard_map/pallas_call | solution.py:127
  133.6 10.1 %shard_map.107.pb_ref = bf16[256,512]{1,0:T(8,128)(2,1)} custom-call(bf16[16,768,256]{2,1,0:T(8,128)(2,1)} %shard_map.106.p_ref, bf16[512,1024]{1,0:T(8,128)(2,1)} %shard_map.104.v_ref.t_ref, bf16[512,1024]{1,0:T(8,128)(2,1)} %shard_map.104.v_ref.t_ref), custom_call_target="tpu_custom_call" | custom-call | tf_op jit(solution)/shard_map/pallas_call | solution.py:183
  143.7 10.1 %shard_map.105.pa_ref = bf16[256,512]{1,0:T(8,128)(2,1)} custom-call(bf16[16,768,256]{2,1,0:T(8,128)(2,1)} %shard_map.103.p_ref, bf16[512,1024]{1,0:T(8,128)(2,1)} %shard_map.104.v_ref.t_ref, bf16[512,1024]{1,0:T(8,128)(2,1)} %shard_map.104.v_ref.t_ref), custom_call_target="tpu_custom_call" | custom-call | tf_op jit(solution)/shard_map/pallas_call | solution.py:183
  153.8 15.9 %shard_map.108 = bf16[64,256,128]{2,1,0:T(8,128)(2,1)} custom-call(bf16[256,512]{1,0:T(8,128)(2,1)} %shard_map.105.pa_ref, bf16[256,512]{1,0:T(8,128)(2,1)} %shard_map.107.pb_ref, bf16[512,8192]{1,0:T(8,128)(2,1)} %xa_ref.1, bf16[512,8192]{1,0:T(8,128)(2,1)} %collective-permute-done.refs_2_.xb_ref), custom_call_target="tpu_custom_call" | custom-call | tf_op jit(solution)/shard_map/pallas_call | solution.py:211
  169.7 7.4 %all-to-all-start = ((bf16[64,256,128]{2,1,0:T(8,128)(2,1)}), bf16[64,256,128]{2,1,0:T(8,128)(2,1)}, u32[]{:S(2)}, u32[]{:S(2)}) async-start(bf16[64,256,128]{2,1,0:T(8,128)(2,1)} %shard_map.108), calls=%async_computation | async-start | bytes 8388608 | tf_op jit(solution)/shard_map/all_to_all | solution.py:298
  178.3 50.1 %all-to-all-done = bf16[64,256,128]{2,1,0:T(8,128)(2,1)} async-done(((bf16[64,256,128]{2,1,0:T(8,128)(2,1)}), bf16[64,256,128]{2,1,0:T(8,128)(2,1)}, u32[]{:S(2)}, u32[]{:S(2)}) %all-to-all-start) | async-done | bytes 4194336 | tf_op jit(solution)/shard_map/all_to_all | solution.py:298
  228.4 2.8 %convert_reduce_fusion = f32[256,128]{1,0:T(8,128)S(1)} fusion(bf16[64,256,128]{2,1,0:T(8,128)(2,1)} %all-to-all-done), kind=kLoop, calls=%fused_computation | loop fusion | flops 4161536 | bytes 4325376 | tf_op jit(solution)/shard_map/reduce_sum | solution.py:300
  231.9 2.6 select_maximum_fusion
  235.1 15.8 %all-to-all-start.1 = ((f32[128,1,128]{2,1,0:T(1,128)}), f32[128,1,128]{2,1,0:T(1,128)S(1)}, u32[]{:S(2)}, u32[]{:S(2)}) async-start(f32[128,1,128]{2,1,0:T(1,128)} %broadcast_in_dim.5), calls=%async_computation.1 | async-start | bytes 131072 | tf_op jit(solution)/shard_map/all_to_all | solution.py:312
  253.1 5.7 %all-to-all-done.1 = f32[128,1,128]{2,1,0:T(1,128)S(1)} async-done(((f32[128,1,128]{2,1,0:T(1,128)}), f32[128,1,128]{2,1,0:T(1,128)S(1)}, u32[]{:S(2)}, u32[]{:S(2)}) %all-to-all-start.1) | async-done | bytes 65568 | tf_op jit(solution)/shard_map/all_to_all | solution.py:312
  (83 shorter events, 34.5 us)
Async XLA Ops:
  0.6 115.6 %collective-permute-start = (bf16[512,8192]{1,0:T(8,128)(2,1)}, bf16[512,8192]{1,0:T(8,128)(2,1)}, u32[]{:S(2)}, u32[]{:S(2)}) collective-permute-start(bf16[512,8192]{1,0:T(8,128)(2,1)} %xa_ref.1), channel_id=1, source_target_pairs={{0,32},{32,0},{1,33},{33,1},{2,34},{34,2},{3,35},{35,3},{4,36},{36... | collective-permute-start | bytes 25165832 | tf_op jit(solution)/shard_map/ppermute | solution.py:291
  2.5 8.8 %collective-permute-start.1 = (bf16[512,256]{1,0:T(8,128)(2,1)S(1)}, bf16[512,256]{1,0:T(8,128)(2,1)S(1)}, u32[]{:S(2)}, u32[]{:S(2)}) collective-permute-start(bf16[512,256]{1,0:T(8,128)(2,1)S(1)} %pad_maximum_fusion.1), channel_id=1, source_target_pairs={{0,65},{65,0},{64,1},{1,64},{2,67},{67,2},{66,3},{3,66},{4,69},{69... | collective-permute-start | bytes 786440 | tf_op jit(solution)/shard_map/ppermute | solution.py:255
  12.0 10.3 %collective-permute-start.10 = (bf16[512,256]{1,0:T(8,128)(2,1)S(1)}, bf16[512,256]{1,0:T(8,128)(2,1)S(1)}, u32[]{:S(2)}, u32[]{:S(2)}) collective-permute-start(bf16[512,256]{1,0:T(8,128)(2,1)S(1)} %pad_maximum_fusion.2), channel_id=1, source_target_pairs={{0,2},{2,4},{4,6},{6,0},{1,3},{3,5},{5,7},{7,1},{8,10},{10,12},{12... | collective-permute-start | bytes 786440 | tf_op jit(solution)/shard_map/ppermute | solution.py:227
  14.0 8.4 %collective-permute-start.11 = (bf16[512,256]{1,0:T(8,128)(2,1)S(1)}, bf16[512,256]{1,0:T(8,128)(2,1)S(1)}, u32[]{:S(2)}, u32[]{:S(2)}) collective-permute-start(bf16[512,256]{1,0:T(8,128)(2,1)S(1)} %pad_maximum_fusion.2), channel_id=1, source_target_pairs={{0,6},{2,0},{4,2},{6,4},{1,7},{3,1},{5,3},{7,5},{8,14},{10,8},{12,... | collective-permute-start | bytes 786440 | tf_op jit(solution)/shard_map/ppermute | solution.py:227
  22.3 6.2 %collective-permute-start.12 = (bf16[256,256]{1,0:T(8,128)(2,1)S(1)}, bf16[256,256]{1,0:T(8,128)(2,1)S(1)}, u32[]{:S(2)}, u32[]{:S(2)}) collective-permute-start(bf16[256,256]{1,0:T(8,128)(2,1)S(1)} %slice.73), channel_id=1, source_target_pairs={{0,2},{2,4},{4,6},{6,0},{1,3},{3,5},{5,7},{7,1},{8,10},{10,12},{12... | collective-permute-start | bytes 393224 | tf_op jit(solution)/shard_map/ppermute | solution.py:227
  22.4 6.8 %collective-permute-start.13 = (bf16[256,256]{1,0:T(8,128)(2,1)S(1)}, bf16[256,256]{1,0:T(8,128)(2,1)S(1)}, u32[]{:S(2)}, u32[]{:S(2)}) collective-permute-start(bf16[256,256]{1,0:T(8,128)(2,1)S(1)} %slice.74), channel_id=1, source_target_pairs={{0,6},{2,0},{4,2},{6,4},{1,7},{3,1},{5,3},{7,5},{8,14},{10,8},{12,... | collective-permute-start | bytes 393224 | tf_op jit(solution)/shard_map/ppermute | solution.py:227
  29.9 38.8 %collective-permute-start.14 = (bf16[2048,256]{1,0:T(8,128)(2,1)}, bf16[2048,256]{1,0:T(8,128)(2,1)}, u32[]{:S(2)}, u32[]{:S(2)}) collective-permute-start(bf16[2048,256]{1,0:T(8,128)(2,1)} %constant_dynamic-update-slice_fusion.6.refs_8_), channel_id=1, source_target_pairs={{0,8},{8,16},{16,24},{24,0},{1,9},{9,17},{17,25},{25,1},{2,10},{10... | collective-permute-start | bytes 3145736 | tf_op jit(solution)/shard_map/ppermute | solution.py:227
  34.6 63.5 %collective-permute-start.18 = (bf16[512,2048]{1,0:T(8,128)(2,1)}, bf16[512,2048]{1,0:T(8,128)(2,1)S(1)}, u32[]{:S(2)}, u32[]{:S(2)}) collective-permute-start(bf16[512,2048]{1,0:T(8,128)(2,1)} %constant_dynamic-slice_fusion.1), channel_id=1, source_target_pairs={{0,32},{32,0},{1,33},{33,1},{2,34},{34,2},{3,35},{35,3},{4,36},{36... | collective-permute-start | bytes 6291464 | tf_op jit(solution)/shard_map/ppermute | solution.py:289
  34.6 25.3 %collective-permute-start.2 = (bf16[512,256]{1,0:T(8,128)(2,1)S(1)}, bf16[512,256]{1,0:T(8,128)(2,1)S(1)}, u32[]{:S(2)}, u32[]{:S(2)}) collective-permute-start(bf16[512,256]{1,0:T(8,128)(2,1)S(1)} %pad_maximum_fusion), channel_id=1, source_target_pairs={{0,8},{8,16},{16,24},{24,0},{1,9},{9,17},{17,25},{25,1},{2,10},{10... | collective-permute-start | bytes 786440 | tf_op jit(solution)/shard_map/ppermute | solution.py:227
  36.2 24.2 %collective-permute-start.3 = (bf16[512,256]{1,0:T(8,128)(2,1)S(1)}, bf16[512,256]{1,0:T(8,128)(2,1)S(1)}, u32[]{:S(2)}, u32[]{:S(2)}) collective-permute-start(bf16[512,256]{1,0:T(8,128)(2,1)S(1)} %pad_maximum_fusion), channel_id=1, source_target_pairs={{0,24},{8,0},{16,8},{24,16},{1,25},{9,1},{17,9},{25,17},{2,26},{10... | collective-permute-start | bytes 786440 | tf_op jit(solution)/shard_map/ppermute | solution.py:227
  60.5 7.6 %collective-permute-start.5 = (bf16[256,256]{1,0:T(8,128)(2,1)S(1)}, bf16[256,256]{1,0:T(8,128)(2,1)S(1)}, u32[]{:S(2)}, u32[]{:S(2)}) collective-permute-start(bf16[256,256]{1,0:T(8,128)(2,1)S(1)} %slice.69), channel_id=1, source_target_pairs={{0,24},{8,0},{16,8},{24,16},{1,25},{9,1},{17,9},{25,17},{2,26},{10... | collective-permute-start | bytes 393224 | tf_op jit(solution)/shard_map/ppermute | solution.py:227
  66.2 21.8 %collective-permute-start.15 = (bf16[2048,256]{1,0:T(8,128)(2,1)}, bf16[2048,256]{1,0:T(8,128)(2,1)}, u32[]{:S(2)}, u32[]{:S(2)}) collective-permute-start(bf16[2048,256]{1,0:T(8,128)(2,1)} %constant_dynamic-update-slice_fusion.6.refs_8_), channel_id=1, source_target_pairs={{0,24},{8,0},{16,8},{24,16},{1,25},{9,1},{17,9},{25,17},{2,26},{10... | collective-permute-start | bytes 3145736 | tf_op jit(solution)/shard_map/ppermute | solution.py:227
  68.7 22.4 %collective-permute-start.6 = (bf16[2048,256]{1,0:T(8,128)(2,1)}, bf16[2048,256]{1,0:T(8,128)(2,1)}, u32[]{:S(2)}, u32[]{:S(2)}) collective-permute-start(bf16[2048,256]{1,0:T(8,128)(2,1)} %constant_dynamic-update-slice_fusion.refs_3_), channel_id=1, source_target_pairs={{0,2},{2,4},{4,6},{6,0},{1,3},{3,5},{5,7},{7,1},{8,10},{10,12},{12... | collective-permute-start | bytes 3145736 | tf_op jit(solution)/shard_map/ppermute | solution.py:227
  68.7 25.8 %collective-permute-start.7 = (bf16[2048,256]{1,0:T(8,128)(2,1)}, bf16[2048,256]{1,0:T(8,128)(2,1)}, u32[]{:S(2)}, u32[]{:S(2)}) collective-permute-start(bf16[2048,256]{1,0:T(8,128)(2,1)} %constant_dynamic-update-slice_fusion.refs_3_), channel_id=1, source_target_pairs={{0,6},{2,0},{4,2},{6,4},{1,7},{3,1},{5,3},{7,5},{8,14},{10,8},{12,... | collective-permute-start | bytes 3145736 | tf_op jit(solution)/shard_map/ppermute | solution.py:227
  88.1 10.0 %collective-permute-start.19 = (bf16[512,256]{1,0:T(8,128)(2,1)S(1)}, bf16[512,256]{1,0:T(8,128)(2,1)S(1)}, u32[]{:S(2)}, u32[]{:S(2)}) collective-permute-start(bf16[512,256]{1,0:T(8,128)(2,1)S(1)} %constant_dynamic-slice_fusion), channel_id=1, source_target_pairs={{0,32},{32,0},{1,33},{33,1},{2,34},{34,2},{3,35},{35,3},{4,36},{36... | collective-permute-start | bytes 786440 | tf_op jit(solution)/shard_map/ppermute | solution.py:290
  91.1 25.1 %collective-permute-start.16 = (bf16[1024,256]{1,0:T(8,128)(2,1)S(1)}, bf16[1024,256]{1,0:T(8,128)(2,1)}, u32[]{:S(2)}, u32[]{:S(2)}) collective-permute-start(bf16[1024,256]{1,0:T(8,128)(2,1)S(1)} %slice.75), channel_id=1, source_target_pairs={{0,8},{8,16},{16,24},{24,0},{1,9},{9,17},{17,25},{25,1},{2,10},{10... | collective-permute-start | bytes 1572872 | tf_op jit(solution)/shard_map/ppermute | solution.py:227
  94.5 21.7 %collective-permute-start.17 = (bf16[1024,256]{1,0:T(8,128)(2,1)S(1)}, bf16[1024,256]{1,0:T(8,128)(2,1)}, u32[]{:S(2)}, u32[]{:S(2)}) collective-permute-start(bf16[1024,256]{1,0:T(8,128)(2,1)S(1)} %slice.76), channel_id=1, source_target_pairs={{0,24},{8,0},{16,8},{24,16},{1,25},{9,1},{17,9},{25,17},{2,26},{10... | collective-permute-start | bytes 1572872 | tf_op jit(solution)/shard_map/ppermute | solution.py:227
  98.1 18.1 %collective-permute-start.8 = (bf16[1024,256]{1,0:T(8,128)(2,1)}, bf16[1024,256]{1,0:T(8,128)(2,1)}, u32[]{:S(2)}, u32[]{:S(2)}) collective-permute-start(bf16[1024,256]{1,0:T(8,128)(2,1)} %slice.70), channel_id=1, source_target_pairs={{0,2},{2,4},{4,6},{6,0},{1,3},{3,5},{5,7},{7,1},{8,10},{10,12},{12... | collective-permute-start | bytes 1572872 | tf_op jit(solution)/shard_map/ppermute | solution.py:227
  98.1 18.1 %collective-permute-start.9 = (bf16[1024,256]{1,0:T(8,128)(2,1)}, bf16[1024,256]{1,0:T(8,128)(2,1)}, u32[]{:S(2)}, u32[]{:S(2)}) collective-permute-start(bf16[1024,256]{1,0:T(8,128)(2,1)} %slice.71), channel_id=1, source_target_pairs={{0,6},{2,0},{4,2},{6,4},{1,7},{3,1},{5,3},{7,5},{8,14},{10,8},{12,... | collective-permute-start | bytes 1572872 | tf_op jit(solution)/shard_map/ppermute | solution.py:227
  169.7 58.6 %all-to-all-start = ((bf16[64,256,128]{2,1,0:T(8,128)(2,1)}), bf16[64,256,128]{2,1,0:T(8,128)(2,1)}, u32[]{:S(2)}, u32[]{:S(2)}) async-start(bf16[64,256,128]{2,1,0:T(8,128)(2,1)} %shard_map.108), calls=%async_computation | async-start | bytes 8388608 | tf_op jit(solution)/shard_map/all_to_all | solution.py:298
  235.1 23.7 %all-to-all-start.1 = ((f32[128,1,128]{2,1,0:T(1,128)}), f32[128,1,128]{2,1,0:T(1,128)S(1)}, u32[]{:S(2)}, u32[]{:S(2)}) async-start(f32[128,1,128]{2,1,0:T(1,128)} %broadcast_in_dim.5), calls=%async_computation.1 | async-start | bytes 131072 | tf_op jit(solution)/shard_map/all_to_all | solution.py:312
  250.9 12.2 %collective-permute-start.20 = (f32[128,256]{0,1:T(8,128)S(1)}, f32[128,256]{0,1:T(8,128)S(1)}, u32[]{:S(2)}, u32[]{:S(2)}) collective-permute-start(f32[128,256]{0,1:T(8,128)S(1)} %get-tuple-element.30), channel_id=1, source_target_pairs={{0,32},{32,0},{1,33},{33,1},{2,34},{34,2},{3,35},{35,3},{4,36},{36... | collective-permute-start | bytes 393224 | tf_op jit(solution)/shard_map/ppermute | solution.py:314
  251.3 11.8 %collective-permute-start.21 = (f32[128,256]{0,1:T(8,128)S(1)}, f32[128,256]{0,1:T(8,128)S(1)}, u32[]{:S(2)}, u32[]{:S(2)}) collective-permute-start(f32[128,256]{0,1:T(8,128)S(1)} %get-tuple-element.30), channel_id=1, source_target_pairs={{0,64},{64,0},{1,65},{65,1},{2,66},{66,2},{3,67},{67,3},{4,68},{68... | collective-permute-start | bytes 393224 | tf_op jit(solution)/shard_map/ppermute | solution.py:315
  252.6 10.5 %collective-permute-start.22 = (f32[128,256]{0,1:T(8,128)S(1)}, f32[128,256]{0,1:T(8,128)S(1)}, u32[]{:S(2)}, u32[]{:S(2)}) collective-permute-start(f32[128,256]{0,1:T(8,128)S(1)} %get-tuple-element.30), channel_id=1, source_target_pairs={{0,96},{32,64},{64,32},{96,0},{1,97},{33,65},{65,33},{97,1},{2,98}... | collective-permute-start | bytes 393224 | tf_op jit(solution)/shard_map/ppermute | solution.py:316
  (7 other events, 163.6 us)

commit v2 on v1

v2 whole, which is shorter than its diff:
```python
import functools
import math

import jax
import jax.numpy as jnp
from jax import lax
from jax.experimental import pallas as pl
from jax.experimental.pallas import tpu as pltpu
from jax.sharding import Mesh, PartitionSpec as P

HD = 128
EPSILON = 1e-05
BF = jnp.bfloat16
F32 = jnp.float32
LEN = 512
HALF = 256
WIDE = 256
PER = 8
VMEM = 56 * 1024 * 1024
NT = (((1,), (1,)), ((), ()))
Y_SWAP = [(0, 3), (3, 0), (2, 1), (1, 2)]


def _params(n):
    return pltpu.CompilerParams(
        dimension_semantics=("arbitrary",) * n, vmem_limit_bytes=VMEM
    )


Q_STEP = 4


def _probs_kernel(off, qa_ref, ka_ref, qb_ref, kb_ref, p0_ref, p1_ref):
    del off
    factor = math.log2(math.e) / math.sqrt(HD)
    rows = lax.broadcasted_iota(jnp.int32, (HALF, HALF), 0)
    cols = lax.broadcasted_iota(jnp.int32, (HALF, HALF), 1)
    seen = rows <= cols

    def go(q_ref, k_ref):
        for j in range(Q_STEP):
            q = q_ref[:, j * HD : (j + 1) * HD]
            out = slice(j * HALF, (j + 1) * HALF)
            diag = lax.dot_general(
                k_ref[:HALF], q[:HALF], NT, preferred_element_type=F32
            )
            diag = jnp.where(seen, diag, -jnp.inf)
            top = jnp.max(diag, axis=0, keepdims=True)
            e = jnp.exp2((diag - top) * factor)
            inv = 1.0 / jnp.sum(e, axis=0, keepdims=True)
            p0_ref[:, out] = (e * inv).astype(BF)
            low = lax.dot_general(
                k_ref[:HALF], q[HALF:], NT, preferred_element_type=F32
            )
            diag = lax.dot_general(
                k_ref[HALF:], q[HALF:], NT, preferred_element_type=F32
            )
            diag = jnp.where(seen, diag, -jnp.inf)
            top = jnp.maximum(
                jnp.max(low, axis=0, keepdims=True),
                jnp.max(diag, axis=0, keepdims=True),
            )
            e = jnp.exp2((low - top) * factor)
            f = jnp.exp2((diag - top) * factor)
            inv = 1.0 / (
                jnp.sum(e, axis=0, keepdims=True) + jnp.sum(f, axis=0, keepdims=True)
            )
            p1_ref[:HALF, out] = (e * inv).astype(BF)
            p1_ref[HALF:, out] = (f * inv).astype(BF)

    @pl.when(pl.program_id(0) == 0)
    def _():
        go(qa_ref, ka_ref)

    @pl.when(pl.program_id(0) == 1)
    def _():
        go(qb_ref, kb_ref)


def probs_of(core, queries, keys, other):
    heads = 2 * PER
    steps = heads // Q_STEP
    per = steps // 2
    wide = Q_STEP * HALF

    def first(s, i):
        return jnp.where(s == 0, i, steps - 1)

    return pl.pallas_call(
        _probs_kernel,
        grid_spec=pltpu.PrefetchScalarGridSpec(
            num_scalar_prefetch=1,
            grid=(2, steps),
            in_specs=[
                pl.BlockSpec(
                    (LEN, Q_STEP * HD), lambda s, i, o: (0, o[0] * steps + first(s, i))
                ),
                pl.BlockSpec((LEN, HD), lambda s, i, o: (0, o[0] * 2 + first(s, i) // per)),
                pl.BlockSpec((LEN, Q_STEP * HD), lambda s, i, o: (0, s * i)),
                pl.BlockSpec((LEN, HD), lambda s, i, o: (0, heads + s * (i // per))),
            ],
            out_specs=[
                pl.BlockSpec((HALF, wide), lambda s, i, o: (0, s * steps + i)),
                pl.BlockSpec((LEN, wide), lambda s, i, o: (0, s * steps + i)),
            ],
        ),
        out_shape=[
            jax.ShapeDtypeStruct((HALF, 2 * heads * HALF), BF),
            jax.ShapeDtypeStruct((LEN, 2 * heads * HALF), BF),
        ],
        compiler_params=_params(2),
        cost_estimate=pl.CostEstimate(
            flops=2 * heads * 3 * HALF * HALF * HD * 2,
            bytes_accessed=2 * heads * (3 * HALF * HALF + LEN * HD) * 2,
            transcendentals=2 * heads * 3 * HALF * HALF,
        ),
    )(core, queries, keys, other, other)


SHARD = 256
P_STEP = 2


def _project_kernel(counts, first, last, where, *refs):
    del where
    xs, refs = refs[: 4 * P_STEP], refs[4 * P_STEP :]
    n = len(counts)
    streams, refs = (refs[:n], refs[n : 2 * n]), refs[2 * n :]
    k = pl.program_id(0)
    acc = refs[-1]

    @pl.when(k == 0)
    def _():
        acc[...] = jnp.zeros_like(acc) if first else refs[0][...]

    at = 0
    for i, count in enumerate(counts):

        @pl.when((k >= at) & (k < at + count))
        def _():
            deep = jnp.concatenate([streams[0][i][...], streams[1][i][...]], axis=0)
            for s in range(2):
                x = jnp.concatenate(
                    [r[...] for r in xs[s * 2 * P_STEP : (s + 1) * 2 * P_STEP]], axis=1
                )
                acc[s * LEN : (s + 1) * LEN] += jnp.dot(
                    x, deep, preferred_element_type=F32
                )

        at += count

    if last:

        @pl.when(k == at - 1)
        def _():
            for s in range(2):
                refs[-2][:, s * LEN : (s + 1) * LEN] = (
                    acc[s * LEN : (s + 1) * LEN].T.astype(BF)
                )


def project(where, xa, xb, a_pieces, b_pieces, before=None, last=False):
    deep = P_STEP * SHARD
    counts = [p.shape[0] // deep for p in a_pieces]
    n = sum(counts)
    first = before is None
    x_specs = [
        pl.BlockSpec(
            (LEN, SHARD), lambda k, w, c=c, j=j: (0, w[(c * n + k) * P_STEP + j])
        )
        for c in range(2)
        for j in range(P_STEP)
    ] * 2
    w_specs = [
        pl.BlockSpec(
            (deep, 2 * WIDE),
            lambda k, w, a=sum(counts[:i]), c=count: (jnp.clip(k - a, 0, c - 1), 0),
        )
        for i, count in enumerate(counts)
    ] * 2
    whole = pl.BlockSpec((2 * LEN, 2 * WIDE), lambda k, w: (0, 0))

    def kernel(*refs):
        _project_kernel(counts, first, last, *refs)

    return pl.pallas_call(
        kernel,
        grid_spec=pltpu.PrefetchScalarGridSpec(
            num_scalar_prefetch=1,
            grid=(n,),
            in_specs=[*x_specs, *w_specs, *([] if first else [whole])],
            out_specs=pl.BlockSpec((2 * WIDE, 2 * LEN), lambda k, w: (0, 0)) if last else whole,
            scratch_shapes=[pltpu.VMEM((2 * LEN, 2 * WIDE), F32)] if last else [],
        ),
        out_shape=jax.ShapeDtypeStruct((2 * WIDE, 2 * LEN), BF)
        if last
        else jax.ShapeDtypeStruct((2 * LEN, 2 * WIDE), F32),
        compiler_params=_params(1),
        cost_estimate=pl.CostEstimate(
            flops=2 * LEN * deep * 2 * n * 2 * WIDE * 2,
            bytes_accessed=n * deep * (4 * LEN + 4 * WIDE) * 2,
            transcendentals=0,
        ),
    )(
        where,
        *[xa] * (2 * P_STEP),
        *[xb] * (2 * P_STEP),
        *a_pieces,
        *b_pieces,
        *([] if first else [before]),
    )


H_STEP = 4


def _pull_kernel(p0_ref, p1_ref, v_ref, t_ref, o_ref, acc):
    h = pl.program_id(2)

    @pl.when(h == 0)
    def _():
        acc[...] = jnp.zeros_like(acc)

    both = jnp.concatenate([v_ref[...], t_ref[...]], axis=0)

    def back(o):
        out, tan = o[:HD], o[HD:]
        square = jnp.sum(out * out, axis=0, keepdims=True) * (1.0 / HD)
        cross = jnp.sum(out * tan, axis=0, keepdims=True) * (1.0 / HD)
        inv2 = 1.0 / (square + EPSILON)
        pull = inv2 * cross * (1.0 + EPSILON * inv2)
        return (inv2 * (tan - out * pull)).astype(BF)

    w0 = back(jnp.dot(both[:, :HALF], p0_ref[...], preferred_element_type=F32))
    w1 = back(jnp.dot(both, p1_ref[...], preferred_element_type=F32))
    acc[:HALF] += lax.dot_general(p0_ref[...], w0, NT, preferred_element_type=F32)
    acc[...] += lax.dot_general(p1_ref[...], w1, NT, preferred_element_type=F32)

    @pl.when(h == PER // H_STEP - 1)
    def _():
        o_ref[...] = acc[...].T.astype(BF)


def pull_back(p0, p1, projected):
    steps = PER // H_STEP
    wide = H_STEP * HALF
    return pl.pallas_call(
        _pull_kernel,
        grid=(2, 2, steps),
        in_specs=[
            pl.BlockSpec((HALF, wide), lambda s, g, h: (0, (s * 2 + g) * steps + h)),
            pl.BlockSpec((LEN, wide), lambda s, g, h: (0, (s * 2 + g) * steps + h)),
            pl.BlockSpec((HD, LEN), lambda s, g, h: (g, s)),
            pl.BlockSpec((HD, LEN), lambda s, g, h: (2 + g, s)),
        ],
        out_specs=pl.BlockSpec((HD, LEN), lambda s, g, h: (g, s)),
        out_shape=jax.ShapeDtypeStruct((WIDE, 2 * LEN), BF),
        scratch_shapes=[pltpu.VMEM((LEN, HD), F32)],
        compiler_params=_params(3),
    )(p0, p1, projected, projected)


G_COLS = 2048
OWN = 128


def _ggn_kernel(pa_ref, pb_ref, xa_ref, xb_ref, o_ref):
    total = jnp.dot(pa_ref[...], xa_ref[...], preferred_element_type=F32)
    total += jnp.dot(pb_ref[...], xb_ref[...], preferred_element_type=F32)
    for j in range(G_COLS // OWN):
        o_ref[j] = total[:, j * OWN : (j + 1) * OWN].astype(BF)


def curvature(pulled, xa, xb):
    depth = xa.shape[1]
    return pl.pallas_call(
        _ggn_kernel,
        grid=(depth // G_COLS,),
        in_specs=[
            pl.BlockSpec((WIDE, LEN), lambda i: (0, 0)),
            pl.BlockSpec((WIDE, LEN), lambda i: (0, 1)),
            pl.BlockSpec((LEN, G_COLS), lambda i: (0, i)),
            pl.BlockSpec((LEN, G_COLS), lambda i: (0, i)),
        ],
        out_specs=pl.BlockSpec((G_COLS // OWN, WIDE, OWN), lambda i: (i, 0, 0)),
        out_shape=jax.ShapeDtypeStruct((depth // OWN, WIDE, OWN), BF),
        compiler_params=_params(1),
    )(pulled, pulled, xa, xb)


ANY = pl.BlockSpec(memory_space=pl.ANY)
WHOLE = pl.BlockSpec(memory_space=pltpu.VMEM)


def narrow(core, value, direction):
    def kernel(core_ref, value_ref, direction_ref, o_ref):
        del core_ref
        o_ref[:, :WIDE] = value_ref[...]
        o_ref[:, WIDE:] = direction_ref[...].astype(BF)

    rows = value.shape[0]
    part = pl.BlockSpec((rows, WIDE), lambda i, c: (0, c[0]))
    return pl.pallas_call(
        kernel,
        grid_spec=pltpu.PrefetchScalarGridSpec(
            num_scalar_prefetch=1,
            grid=(1,),
            in_specs=[part, part],
            out_specs=pl.BlockSpec((rows, 2 * WIDE), lambda i, c: (0, 0)),
        ),
        out_shape=jax.ShapeDtypeStruct((rows, 2 * WIDE), BF),
        compiler_params=_params(1),
    )(core, value, direction)


def chosen(yh, own, swapped, after):
    def kernel(yh_ref, own_ref, swapped_ref, _, low_ref, high_ref, zero_ref):
        zero_ref[0] = 0

        @pl.when(yh_ref[0] == 0)
        def _():
            low_ref[...] = own_ref[...]
            high_ref[...] = swapped_ref[...]

        @pl.when(yh_ref[0] != 0)
        def _():
            low_ref[...] = swapped_ref[...]
            high_ref[...] = own_ref[...]

    return pl.pallas_call(
        kernel,
        in_specs=[pl.BlockSpec(memory_space=pltpu.SMEM), WHOLE, WHOLE, ANY],
        out_specs=[WHOLE, WHOLE, pl.BlockSpec(memory_space=pltpu.SMEM)],
        out_shape=[jax.ShapeDtypeStruct(own.shape, BF)] * 2
        + [jax.ShapeDtypeStruct((1,), jnp.int32)],
        compiler_params=pltpu.CompilerParams(vmem_limit_bytes=VMEM),
    )(yh, own, swapped, after)


def halves(arrays, after):
    n = len(arrays)
    half = arrays[0].shape[0] // 2
    steps = max(half // 256, 1)
    rows = half // steps

    def kernel(*refs):
        for a, o in zip(refs[:n], refs[-n:]):
            o[...] = a[...]

    shape = (rows, arrays[0].shape[1])
    return pl.pallas_call(
        kernel,
        grid=(steps,),
        in_specs=[
            pl.BlockSpec(shape, lambda i, c=c % 2: (i + c * steps, 0)) for c in range(n)
        ]
        + [ANY] * len(after),
        out_specs=[pl.BlockSpec(shape, lambda i: (i, 0))] * n,
        out_shape=[jax.ShapeDtypeStruct((half, shape[1]), BF)] * n,
        compiler_params=_params(1),
    )(*arrays, *after)


def joined(lists):
    flat = sum(lists, [])

    def kernel(*refs):
        at = 0
        for arrays, o in zip(lists, refs[len(flat) :]):
            row = 0
            for _ in arrays:
                n = refs[at].shape[0]
                o[row : row + n] = refs[at][...]
                row, at = row + n, at + 1

    return pl.pallas_call(
        kernel,
        in_specs=[WHOLE] * len(flat),
        out_specs=[WHOLE] * len(lists),
        out_shape=[
            jax.ShapeDtypeStruct((sum(a.shape[0] for a in l), l[0].shape[1]), BF)
            for l in lists
        ],
        compiler_params=pltpu.CompilerParams(vmem_limit_bytes=VMEM),
    )(*flat)


def hop(x, axis, by):
    return lax.ppermute(x, axis, [(i, (i + by) % 4) for i in range(4)])


def rings(arrays, axes, after):
    near = [hop(x, a, by) for x, a in zip(arrays, axes) for by in (1, 3)]
    cut = halves(near, after)
    far = [hop(h, axes[i // 2], (1, 3)[i % 2]) for i, h in enumerate(cut)]
    return [(x, *near[2 * i : 2 * i + 2], *far[2 * i : 2 * i + 2]) for i, x in enumerate(arrays)]


S_STEP = 16


def _share_kernel(at_ref, damping_ref, parts_ref, d_ref, r_ref, h_ref, row_ref, acc, *, tokens):
    del at_ref
    i = pl.program_id(0)

    @pl.when(i == 0)
    def _():
        acc[...] = jnp.zeros_like(acc)

    acc[...] += jnp.sum(parts_ref[...].astype(F32), axis=0)

    @pl.when(i == pl.num_programs(0) - 1)
    def _():
        d, r = d_ref[...], r_ref[...]
        h = acc[...].T * (1.0 / tokens) + damping_ref[0] * d
        h_ref[...] = h
        lane = lax.broadcasted_iota(jnp.int32, row_ref.shape, 1)
        row = jnp.zeros(row_ref.shape, F32)
        for j, term in enumerate((r * r, d * h, r * h, h * h)):
            row = jnp.where(lane == j, jnp.sum(term), row)
        row_ref[...] = row


def share(at, damping, parts, direction, residual, devices, tokens):
    n = parts.shape[0] // S_STEP
    own = pl.BlockSpec((OWN, WIDE), lambda i, w: (w[0], w[1]))
    return pl.pallas_call(
        functools.partial(_share_kernel, tokens=tokens),
        grid_spec=pltpu.PrefetchScalarGridSpec(
            num_scalar_prefetch=1,
            grid=(n,),
            in_specs=[
                pl.BlockSpec(memory_space=pltpu.SMEM),
                pl.BlockSpec((S_STEP, WIDE, OWN), lambda i, w: (i, 0, 0)),
                own,
                own,
            ],
            out_specs=[
                pl.BlockSpec((OWN, WIDE), lambda i, w: (0, 0)),
                pl.BlockSpec((devices, 128), lambda i, w: (0, 0)),
            ],
            scratch_shapes=[pltpu.VMEM((WIDE, OWN), F32)],
        ),
        out_shape=[
            jax.ShapeDtypeStruct((OWN, WIDE), F32),
            jax.ShapeDtypeStruct((devices, 128), F32),
        ],
        compiler_params=_params(1),
    )(at, damping, parts, direction, residual)


CHIPS = ("x", "z", "yh", "yl")


def body(normed, queries, keys, value_weight, iterate, residual, direction, damping):
    core, yl = lax.axis_index("c"), lax.axis_index("yl")
    x, z, yh = (lax.axis_index(a) for a in ("x", "z", "yh"))
    other = 1 - core
    swap = [(0, 1), (1, 0)]
    heads = 2 * PER * HD

    def cols(a, which, width):
        return lax.dynamic_slice_in_dim(a, which * width, width, 1)

    own = narrow(core[None], value_weight, direction)
    normed_b = lax.ppermute(normed, "c", swap)
    swapped = lax.ppermute(own, ("yl", "yh"), Y_SWAP)
    *near, _ = chosen(yh[None], own, swapped, own)
    *far, zero = chosen(yh[None], own, swapped, normed_b)
    later = other + zero[0]
    partner = jnp.concatenate([cols(queries, later, heads), cols(keys, later, WIDE)], 1)
    partner = lax.ppermute(partner, "c", swap)
    inner = [
        [a, hop(a, axis, 1), hop(a, axis, 3), hop(b, axis, 2)]
        for a, b, axis in zip(near, far, "xz")
    ]
    lines = joined(inner)
    p0, p1 = probs_of(core[None], queries, keys, partner)
    turn = (0, -1, 1, 2)

    def places(steps):
        a_at = [((x + i) % 4) * 8 + (z + s) % 4 * 2 for s in steps for i in turn]
        b_at = [((x + s) % 4) * 8 + (z + i) % 4 * 2 + 1 for s in steps for i in turn]
        return jnp.stack(a_at + b_at).astype(jnp.int32)

    some = project(places((0,)), normed, normed_b, lines[:1], lines[1:])
    (_, *a, a_far, a_far2), (_, *b, b_far, b_far2) = rings(lines, "zx", [p0, some])
    most = project(places((-1, 1)), normed, normed_b, a, b, some)
    projected = project(
        places((2,)), normed, normed_b, [a_far, a_far2], [b_far, b_far2], most, True
    )
    pulled = pull_back(p0, p1, projected)
    parts = curvature(pulled, normed, normed_b)
    parts = lax.all_to_all(parts, CHIPS, 0, 0, tiled=True)
    everyone = ("c",) + CHIPS
    devices = lax.axis_size(everyone)
    h, rows = share(
        jnp.stack([yl, core]), damping, parts, direction, residual, devices, devices * normed.shape[0]
    )
    rows = lax.all_to_all(rows, everyone, 0, 0, tiled=True)
    total = jnp.sum(rows, axis=0)
    h_c = lax.ppermute(h, "c", swap)
    h_y = lax.ppermute(h, "yl", swap)
    h_yc = lax.ppermute(h, ("yl", "c"), [(i, 3 - i) for i in range(4)])

    def in_order(flag, a, b, axis):
        return jnp.where(
            flag == 0, jnp.concatenate([a, b], axis), jnp.concatenate([b, a], axis)
        )

    hdir = in_order(yl, in_order(core, h, h_c, 1), in_order(core, h_y, h_yc, 1), 0)
    rr, ph, rh, hh = total[0], total[1], total[2], total[3]
    step = rr / ph
    nn = rr - 2.0 * step * rh + step * step * hh
    new_iterate = iterate + step * direction
    new_residual = residual - step * hdir
    new_direction = new_residual + nn / rr * direction
    return (new_iterate, new_residual, new_direction)


def solution(mesh):
    fine = Mesh(
        mesh.devices.reshape(2, 2, 4, 4, 2), ("yl", "c", "x", "z", "yh")
    )
    tokens = P(("yl", "c", "x", "z", "yh"), None)
    rows = P(("x", "z", "yh"), None)
    return jax.shard_map(
        body,
        mesh=fine,
        in_specs=(tokens, tokens, tokens, rows, rows, rows, rows, P()),
        out_specs=(rows, rows, rows),
        check_vma=False,
    )
```

time: 270 us -> 221 us (0.82)
  waiting for transfers between devices: 113 us -> 72.1 us
  local copies, waits for them, and re-layouts: 22.7 us -> 8.14 us
  Pallas kernels: 67.7 us -> 77.6 us
  starting transfers between devices: 51.7 us -> 49 us
    ppermute x16 -> x14, waiting for transfers between devices: 48.6 us -> 9.14 us  [hop(): return lax.ppermute(x, axis, [(i, (i + by) % 4) for i in range(4)])]
    pallas_call x1 -> x3, Pallas kernels: 17.4 us -> 26 us  [project(): pl.pallas_call(kernel, grid_spec=pltpu.PrefetchScalarGridSpec(num_scalar_...]
    pallas_call x2 -> x7, Pallas kernels: 20.2 us -> 28.1 us  [the longest x1 12.2 us: pull_back(): pl.pallas_call(_pull_kernel, grid=(2, 2, steps), in_specs=[pl.BlockSpec((...]
    slice x9 -> x0, local copies, waits for them, and re-layouts: 6.66 us -> none  [the longest x4 2.96 us: ring(): far_b = hop(after[half:], axis, 3)]
    unnamed x25 -> x40, local copies, waits for them, and re-layouts: 9.58 us -> 3.71 us
    pallas_call x1, Pallas kernels: 15.9 us -> 10.2 us  [curvature(): pl.pallas_call(_ggn_kernel, grid=(depth // G_COLS,), in_specs=[pl.BlockSp...]
    all_to_all x1, waiting for transfers between devices: 50.1 us -> 46 us  [body(): parts = lax.all_to_all(parts, CHIPS, 0, 0, tiled=True)]
    reduce_sum x2 -> x0, other arithmetic: 3.49 us -> none  [the longest x1 2.79 us: body(): summed = jnp.sum(parts.astype(F32), axis=0).T]
  transfers between devices with their start and end apart: 25 -> 22, of which waited for: 9 -> 8; matrix products, arithmetic and copies ran while one was open for 7% -> 2% of each run, Pallas kernels for 5% -> 17%
where the time goes in v2:
time: 221 us; the launch traced here: 218 us
  Pallas kernels  77.6 us (35%)
  waiting for transfers between devices  72.1 us (33%)
  starting transfers between devices  49 us (22%)
  local copies, waits for them, and re-layouts  8.14 us (4%)
  between operations  6.18 us (3%)
  other arithmetic  4.67 us (2%)
    all_to_all x1, waiting for transfers between devices, body(): parts = lax.all_to_all(parts, CHIPS, 0, 0, tiled=True)  46 us
    ppermute x14, starting transfers between devices, hop(): return lax.ppermute(x, axis, [(i, (i + by) % 4) for i in range(4)])  26.2 us
    pallas_call x3, Pallas kernels, project(): pl.pallas_call(kernel, grid_spec=pltpu.PrefetchScalarGridSpec(num_scalar_...  26 us
    all_to_all x1, starting transfers between devices, body(): rows = lax.all_to_all(rows, everyone, 0, 0, tiled=True)  14.1 us
    pallas_call x1, Pallas kernels, probs_of(): pl.pallas_call(_probs_kernel, grid_spec=pltpu.PrefetchScalarGridSpec(num_...  13.3 us
    pallas_call x1, Pallas kernels, pull_back(): pl.pallas_call(_pull_kernel, grid=(2, 2, steps), in_specs=[pl.BlockSpec((...  12.2 us
    pallas_call x1, Pallas kernels, curvature(): pl.pallas_call(_ggn_kernel, grid=(depth // G_COLS,), in_specs=[pl.BlockSp...  10.2 us
    ppermute x14, waiting for transfers between devices, hop(): return lax.ppermute(x, axis, [(i, (i + by) % 4) for i in range(4)])  9.14 us
  transfers between devices with their start and end apart: 22, of which 8 were waited for; matrix products, arithmetic and copies ran while one was open for 2% of the time, Pallas kernels for 17%

profile of v2, /device:TPU:16, one launch (start us, length us, event | category | flops | bytes accessed | tf_op | source)
XLA Modules:
  0.0 217.7 jit_solution(7723097083486284087)
XLA Ops:
  2.9 8.5 %collective-permute-done.swapped_ref = bf16[256,512]{1,0:T(8,128)(2,1)S(1)} collective-permute-done((bf16[256,512]{1,0:T(8,128)(2,1)}, bf16[256,512]{1,0:T(8,128)(2,1)S(1)}, u32[]{:S(2)}, u32[]{:S(2)}) %collective-permute-start) | collective-permute-done | bytes 262176 | tf_op jit(solution)/shard_map/ppermute | solution.py:467
  11.4 2.8 %collective-permute-done.1._.refs_5_.refs_6_.refs_7_.refs_8_.xb_ref = bf16[512,8192]{1,0:T(8,128)(2,1)} collective-permute-done((bf16[512,8192]{1,0:T(8,128)(2,1)}, bf16[512,8192]{1,0:T(8,128)(2,1)}, u32[]{:S(2)}, u32[]{:S(2)}) %collective-permute-start.1) | collective-permute-done | bytes 8388640 | tf_op jit(solution)/shard_map/ppermute | solution.py:466
  27.5 2.1 collective-permute-start.7
  29.6 2.7 %collective-permute-done.3.refs_1_ = bf16[256,512]{1,0:T(8,128)(2,1)S(1)} collective-permute-done((bf16[256,512]{1,0:T(8,128)(2,1)}, bf16[256,512]{1,0:T(8,128)(2,1)S(1)}, u32[]{:S(2)}, u32[]{:S(2)}) %collective-permute-start.3) | collective-permute-done | bytes 262176 | tf_op jit(solution)/shard_map/ppermute | solution.py:389
  34.2 4.0 %collective-permute-start.8 = (bf16[256,512]{1,0:T(8,128)(2,1)S(1)}, bf16[256,512]{1,0:T(8,128)(2,1)S(1)}, u32[]{:S(2)}, u32[]{:S(2)}) collective-permute-start(bf16[256,512]{1,0:T(8,128)(2,1)S(1)} %copy-done.18), channel_id=1, source_target_pairs={{0,4},{2,6},{4,0},{6,2},{1,5},{3,7},{5,1},{7,3},{8,12},{10,14},{12... | collective-permute-start | bytes 786440 | tf_op jit(solution)/shard_map/ppermute | solution.py:389
  38.1 3.5 %collective-permute-done.5.refs_3_ = bf16[256,512]{1,0:T(8,128)(2,1)S(1)} collective-permute-done((bf16[256,512]{1,0:T(8,128)(2,1)S(1)}, bf16[256,512]{1,0:T(8,128)(2,1)S(1)}, u32[]{:S(2)}, u32[]{:S(2)}) %collective-permute-start.5) | collective-permute-done | bytes 262176 | tf_op jit(solution)/shard_map/ppermute | solution.py:389
  41.6 2.2 %collective-permute-done.8.refs_7_ = bf16[256,512]{1,0:T(8,128)(2,1)S(1)} collective-permute-done((bf16[256,512]{1,0:T(8,128)(2,1)S(1)}, bf16[256,512]{1,0:T(8,128)(2,1)S(1)}, u32[]{:S(2)}, u32[]{:S(2)}) %collective-permute-start.8) | collective-permute-done | bytes 262176 | tf_op jit(solution)/shard_map/ppermute | solution.py:389
  44.6 2.9 %shard_map.107 = (bf16[1024,512]{1,0:T(8,128)(2,1)}, bf16[1024,512]{1,0:T(8,128)(2,1)}) custom-call(bf16[256,512]{1,0:T(8,128)(2,1)} %get-tuple-element.21.refs_0_, bf16[256,512]{1,0:T(8,128)(2,1)} %copy-done.11, bf16[256,512]{1,0:T(8,128)(2,1)} %copy-done.12, bf16[256,512]{1,0:T(8,128)(2,1)} %copy-done.15, bf16[256,512]{1,0:T(8,128)(2,1)} %get-tuple-element.23.refs_4_, ...), custom_call_target="tpu_custom_call" | custom-call | tf_op jit(solution)/shard_map/pallas_call | solution.py:376
  48.8 2.1 collective-permute-start.10
  51.6 2.6 %collective-permute-start.12 = (bf16[1024,512]{1,0:T(8,128)(2,1)}, bf16[1024,512]{1,0:T(8,128)(2,1)}, u32[]{:S(2)}, u32[]{:S(2)}) collective-permute-start(bf16[1024,512]{1,0:T(8,128)(2,1)} %get-tuple-element.26.refs_10_), channel_id=1, source_target_pairs={{0,24},{8,0},{16,8},{24,16},{1,25},{9,1},{17,9},{25,17},{2,26},{10... | collective-permute-start | bytes 3145736 | tf_op jit(solution)/shard_map/ppermute | solution.py:389
  54.8 6.7 %shard_map.108.refs_5_.refs_13_ = f32[1024,512]{1,0:T(8,128)} custom-call(s32[8]{0:T(128)} %stack.134.refs_0_, bf16[512,8192]{1,0:T(8,128)(2,1)} %xa_ref.1, bf16[512,8192]{1,0:T(8,128)(2,1)} %xa_ref.1, bf16[512,8192]{1,0:T(8,128)(2,1)} %xa_ref.1, bf16[512,8192]{1,0:T(8,128)(2,1)} %xa_ref.1, ...), custom_call_target="tpu_custom_call" | custom-call | flops 2147483648 | bytes 6291456 | tf_op jit(solution)/shard_map/pallas_call | solution.py:186
  61.5 13.3 %shard_map.105 = (bf16[256,8192]{1,0:T(8,128)(2,1)}, bf16[512,8192]{1,0:T(8,128)(2,1)}) custom-call(s32[1]{0:T(128)} %bitcast.1.core_ref.off, bf16[512,4096]{1,0:T(8,128)(2,1)} %qa_ref.1, bf16[512,512]{1,0:T(8,128)(2,1)} %ka_ref.1, bf16[512,2304]{1,0:T(8,128)(2,1)} %collective-permute-done.2.qb_ref.kb_ref, bf16[512,2304]{1,0:T(8,128)(2,1)} %collective-permute-done.2.qb_ref.kb_ref), custom_call_target="tpu_custom_call" | custom-call | flops 1610612736 | bytes 16777216 | tf_op jit(solution)/shard_map/pallas_call | solution.py:89
  76.6 2.6 %shard_map.109 = (bf16[512,512]{1,0:T(8,128)(2,1)}, bf16[512,512]{1,0:T(8,128)(2,1)}, bf16[512,512]{1,0:T(8,128)(2,1)}, bf16[512,512]{1,0:T(8,128)(2,1)}) custom-call(bf16[1024,512]{1,0:T(8,128)(2,1)} %copy-done.1, bf16[1024,512]{1,0:T(8,128)(2,1)} %copy-done.2, bf16[1024,512]{1,0:T(8,128)(2,1)} %copy-done.3, ...), custom_call_target="tpu_custom_call" | custom-call | tf_op jit(solution)/shard_map/pallas_call | solution.py:351
  79.1 3.2 %collective-permute-start.14 = (bf16[512,512]{1,0:T(8,128)(2,1)}, bf16[512,512]{1,0:T(8,128)(2,1)S(1)}, u32[]{:S(2)}, u32[]{:S(2)}) collective-permute-start(bf16[512,512]{1,0:T(8,128)(2,1)} %get-tuple-element.28), channel_id=1, source_target_pairs={{0,6},{2,0},{4,2},{6,4},{1,7},{3,1},{5,3},{7,5},{8,14},{10,8},{12,... | collective-permute-start | bytes 1572872 | tf_op jit(solution)/shard_map/ppermute | solution.py:389
  82.4 3.2 %collective-permute-start.16 = (bf16[512,512]{1,0:T(8,128)(2,1)}, bf16[512,512]{1,0:T(8,128)(2,1)S(1)}, u32[]{:S(2)}, u32[]{:S(2)}) collective-permute-start(bf16[512,512]{1,0:T(8,128)(2,1)} %get-tuple-element.30), channel_id=1, source_target_pairs={{0,24},{8,0},{16,8},{24,16},{1,25},{9,1},{17,9},{25,17},{2,26},{10... | collective-permute-start | bytes 1572872 | tf_op jit(solution)/shard_map/ppermute | solution.py:389
  86.9 11.2 %shard_map.110.refs_13_ = f32[1024,512]{1,0:T(8,128)} custom-call(s32[16]{0:T(128)} %stack.151.refs_0_, bf16[512,8192]{1,0:T(8,128)(2,1)} %xa_ref.1, bf16[512,8192]{1,0:T(8,128)(2,1)} %xa_ref.1, bf16[512,8192]{1,0:T(8,128)(2,1)} %xa_ref.1, bf16[512,8192]{1,0:T(8,128)(2,1)} %xa_ref.1, ...), custom_call_target="tpu_custom_call" | custom-call | flops 4294967296 | bytes 12582912 | tf_op jit(solution)/shard_map/pallas_call | solution.py:186
  100.1 8.1 %shard_map.111.v_ref.t_ref = bf16[512,1024]{1,0:T(8,128)(2,1)} custom-call(s32[8]{0:T(128)} %stack.125.refs_0_, bf16[512,8192]{1,0:T(8,128)(2,1)} %xa_ref.1, bf16[512,8192]{1,0:T(8,128)(2,1)} %xa_ref.1, bf16[512,8192]{1,0:T(8,128)(2,1)} %xa_ref.1, bf16[512,8192]{1,0:T(8,128)(2,1)} %xa_ref.1, ...), custom_call_target="tpu_custom_call" | custom-call | flops 2147483648 | bytes 6291456 | tf_op jit(solution)/shard_map/pallas_call | solution.py:186
  108.2 12.2 %shard_map.112.pa_ref.pb_ref = bf16[256,1024]{1,0:T(8,128)(2,1)} custom-call(bf16[256,8192]{1,0:T(8,128)(2,1)} %get-tuple-element.19.refs_4_.p0_ref, bf16[512,8192]{1,0:T(8,128)(2,1)} %get-tuple-element.20.p1_ref, bf16[512,1024]{1,0:T(8,128)(2,1)} %shard_map.111.v_ref.t_ref, bf16[512,1024]{1,0:T(8,128)(2,1)} %shard_map.111.v_ref.t_ref), custom_call_target="tpu_custom_call" | custom-call | tf_op jit(solution)/shard_map/pallas_call | solution.py:247
  120.4 10.2 %shard_map.113 = bf16[64,256,128]{2,1,0:T(8,128)(2,1)} custom-call(bf16[256,1024]{1,0:T(8,128)(2,1)} %shard_map.112.pa_ref.pb_ref, bf16[256,1024]{1,0:T(8,128)(2,1)} %shard_map.112.pa_ref.pb_ref, bf16[512,8192]{1,0:T(8,128)(2,1)} %xa_ref.1, bf16[512,8192]{1,0:T(8,128)(2,1)} %collective-permute-done.1._.refs_5_.refs_6_.refs_7_.refs_8_.xb_ref), custom_call_target="tpu_custom_call" | custom-call | tf_op jit(solution)/shard_map/pallas_call | solution.py:276
  130.6 5.8 %all-to-all-start = ((bf16[64,256,128]{2,1,0:T(8,128)(2,1)}), bf16[64,256,128]{2,1,0:T(8,128)(2,1)}, u32[]{:S(2)}, u32[]{:S(2)}) async-start(bf16[64,256,128]{2,1,0:T(8,128)(2,1)} %shard_map.113), calls=%async_computation | async-start | bytes 8388608 | tf_op jit(solution)/shard_map/all_to_all | solution.py:494
  137.8 46.0 %all-to-all-done.parts_ref = bf16[64,256,128]{2,1,0:T(8,128)(2,1)} async-done(((bf16[64,256,128]{2,1,0:T(8,128)(2,1)}), bf16[64,256,128]{2,1,0:T(8,128)(2,1)}, u32[]{:S(2)}, u32[]{:S(2)}) %all-to-all-start) | async-done | bytes 4194336 | tf_op jit(solution)/shard_map/all_to_all | solution.py:494
  183.8 4.8 %shard_map.114 = (f32[128,256]{1,0:T(8,128)}, f32[128,128]{1,0:T(8,128)}) custom-call(s32[2]{0:T(128)} %pad_add_fusion.at_ref, f32[1]{0:T(128)S(6)} %copy.12.damping_ref, bf16[64,256,128]{2,1,0:T(8,128)(2,1)} %all-to-all-done.parts_ref, f32[256,512]{1,0:T(8,128)} %d_ref.1, f32[256,512]{1,0:T(8,128)} %r_ref.1), custom_call_target="tpu_custom_call" | custom-call | tf_op jit(solution)/shard_map/pallas_call | solution.py:427
  188.7 14.1 %all-to-all-start.1 = ((f32[128,1,128]{2,1,0:T(1,128)}), f32[128,1,128]{2,1,0:T(1,128)S(1)}, u32[]{:S(2)}, u32[]{:S(2)}) async-start(f32[128,1,128]{2,1,0:T(1,128)} %bitcast.43), calls=%async_computation.1 | async-start | bytes 131072 | tf_op jit(solution)/shard_map/all_to_all | solution.py:500
  204.9 5.7 %all-to-all-done.1 = f32[128,1,128]{2,1,0:T(1,128)S(1)} async-done(((f32[128,1,128]{2,1,0:T(1,128)}), f32[128,1,128]{2,1,0:T(1,128)S(1)}, u32[]{:S(2)}, u32[]{:S(2)}) %all-to-all-start.1) | async-done | bytes 65568 | tf_op jit(solution)/shard_map/all_to_all | solution.py:500
  (84 shorter events, 30.9 us)
Async XLA Ops:
  0.6 13.6 %collective-permute-start.1 = (bf16[512,8192]{1,0:T(8,128)(2,1)}, bf16[512,8192]{1,0:T(8,128)(2,1)}, u32[]{:S(2)}, u32[]{:S(2)}) collective-permute-start(bf16[512,8192]{1,0:T(8,128)(2,1)} %xa_ref.1), channel_id=1, source_target_pairs={{0,32},{32,0},{1,33},{33,1},{2,34},{34,2},{3,35},{35,3},{4,36},{36... | collective-permute-start | bytes 25165832 | tf_op jit(solution)/shard_map/ppermute | solution.py:466
  2.5 8.9 %collective-permute-start = (bf16[256,512]{1,0:T(8,128)(2,1)}, bf16[256,512]{1,0:T(8,128)(2,1)S(1)}, u32[]{:S(2)}, u32[]{:S(2)}) collective-permute-start(bf16[256,512]{1,0:T(8,128)(2,1)} %shard_map.103.own_ref._), channel_id=1, source_target_pairs={{0,65},{65,0},{64,1},{1,64},{2,67},{67,2},{66,3},{3,66},{4,69},{69... | collective-permute-start | bytes 786440 | tf_op jit(solution)/shard_map/ppermute | solution.py:467
  20.2 41.3 %collective-permute-start.2 = (bf16[512,2304]{1,0:T(8,128)(2,1)}, bf16[512,2304]{1,0:T(8,128)(2,1)}, u32[]{:S(2)}, u32[]{:S(2)}) collective-permute-start(bf16[512,2304]{1,0:T(8,128)(2,1)} %pad_maximum_fusion), channel_id=1, source_target_pairs={{0,32},{32,0},{1,33},{33,1},{2,34},{34,2},{3,35},{35,3},{4,36},{36... | collective-permute-start | bytes 7077896 | tf_op jit(solution)/shard_map/ppermute | solution.py:472
  22.3 10.1 %collective-permute-start.3 = (bf16[256,512]{1,0:T(8,128)(2,1)}, bf16[256,512]{1,0:T(8,128)(2,1)S(1)}, u32[]{:S(2)}, u32[]{:S(2)}) collective-permute-start(bf16[256,512]{1,0:T(8,128)(2,1)} %get-tuple-element.21.refs_0_), channel_id=1, source_target_pairs={{0,8},{8,16},{16,24},{24,0},{1,9},{9,17},{17,25},{25,1},{2,10},{10... | collective-permute-start | bytes 786440 | tf_op jit(solution)/shard_map/ppermute | solution.py:389
  23.8 10.3 %collective-permute-start.4 = (bf16[256,512]{1,0:T(8,128)(2,1)}, bf16[256,512]{1,0:T(8,128)(2,1)S(1)}, u32[]{:S(2)}, u32[]{:S(2)}) collective-permute-start(bf16[256,512]{1,0:T(8,128)(2,1)} %get-tuple-element.21.refs_0_), channel_id=1, source_target_pairs={{0,24},{8,0},{16,8},{24,16},{1,25},{9,1},{17,9},{25,17},{2,26},{10... | collective-permute-start | bytes 786440 | tf_op jit(solution)/shard_map/ppermute | solution.py:389
  25.6 12.5 %collective-permute-start.6 = (bf16[256,512]{1,0:T(8,128)(2,1)}, bf16[256,512]{1,0:T(8,128)(2,1)S(1)}, u32[]{:S(2)}, u32[]{:S(2)}) collective-permute-start(bf16[256,512]{1,0:T(8,128)(2,1)} %get-tuple-element.23.refs_4_), channel_id=1, source_target_pairs={{0,2},{2,4},{4,6},{6,0},{1,3},{3,5},{5,7},{7,1},{8,10},{10,12},{12... | collective-permute-start | bytes 786440 | tf_op jit(solution)/shard_map/ppermute | solution.py:389
  27.5 10.6 %collective-permute-start.7 = (bf16[256,512]{1,0:T(8,128)(2,1)}, bf16[256,512]{1,0:T(8,128)(2,1)S(1)}, u32[]{:S(2)}, u32[]{:S(2)}) collective-permute-start(bf16[256,512]{1,0:T(8,128)(2,1)} %get-tuple-element.23.refs_4_), channel_id=1, source_target_pairs={{0,6},{2,0},{4,2},{6,4},{1,7},{3,1},{5,3},{7,5},{8,14},{10,8},{12,... | collective-permute-start | bytes 786440 | tf_op jit(solution)/shard_map/ppermute | solution.py:389
  32.4 9.3 %collective-permute-start.5 = (bf16[256,512]{1,0:T(8,128)(2,1)S(1)}, bf16[256,512]{1,0:T(8,128)(2,1)S(1)}, u32[]{:S(2)}, u32[]{:S(2)}) collective-permute-start(bf16[256,512]{1,0:T(8,128)(2,1)S(1)} %copy-done.19), channel_id=1, source_target_pairs={{0,16},{8,24},{16,0},{24,8},{1,17},{9,25},{17,1},{25,9},{2,18},{10... | collective-permute-start | bytes 786440 | tf_op jit(solution)/shard_map/ppermute | solution.py:389
  34.2 9.7 %collective-permute-start.8 = (bf16[256,512]{1,0:T(8,128)(2,1)S(1)}, bf16[256,512]{1,0:T(8,128)(2,1)S(1)}, u32[]{:S(2)}, u32[]{:S(2)}) collective-permute-start(bf16[256,512]{1,0:T(8,128)(2,1)S(1)} %copy-done.18), channel_id=1, source_target_pairs={{0,4},{2,6},{4,0},{6,2},{1,5},{3,7},{5,1},{7,3},{8,12},{10,14},{12... | collective-permute-start | bytes 786440 | tf_op jit(solution)/shard_map/ppermute | solution.py:389
  47.6 27.3 %collective-permute-start.9 = (bf16[1024,512]{1,0:T(8,128)(2,1)}, bf16[1024,512]{1,0:T(8,128)(2,1)S(1)}, u32[]{:S(2)}, u32[]{:S(2)}) collective-permute-start(bf16[1024,512]{1,0:T(8,128)(2,1)} %get-tuple-element.25.refs_9_), channel_id=1, source_target_pairs={{0,2},{2,4},{4,6},{6,0},{1,3},{3,5},{5,7},{7,1},{8,10},{10,12},{12... | collective-permute-start | bytes 3145736 | tf_op jit(solution)/shard_map/ppermute | solution.py:389
  48.8 26.0 %collective-permute-start.10 = (bf16[1024,512]{1,0:T(8,128)(2,1)}, bf16[1024,512]{1,0:T(8,128)(2,1)S(1)}, u32[]{:S(2)}, u32[]{:S(2)}) collective-permute-start(bf16[1024,512]{1,0:T(8,128)(2,1)} %get-tuple-element.25.refs_9_), channel_id=1, source_target_pairs={{0,6},{2,0},{4,2},{6,4},{1,7},{3,1},{5,3},{7,5},{8,14},{10,8},{12,... | collective-permute-start | bytes 3145736 | tf_op jit(solution)/shard_map/ppermute | solution.py:389
  51.0 24.6 %collective-permute-start.11 = (bf16[1024,512]{1,0:T(8,128)(2,1)}, bf16[1024,512]{1,0:T(8,128)(2,1)S(1)}, u32[]{:S(2)}, u32[]{:S(2)}) collective-permute-start(bf16[1024,512]{1,0:T(8,128)(2,1)} %get-tuple-element.26.refs_10_), channel_id=1, source_target_pairs={{0,8},{8,16},{16,24},{24,0},{1,9},{9,17},{17,25},{25,1},{2,10},{10... | collective-permute-start | bytes 3145736 | tf_op jit(solution)/shard_map/ppermute | solution.py:389
  51.6 24.0 %collective-permute-start.12 = (bf16[1024,512]{1,0:T(8,128)(2,1)}, bf16[1024,512]{1,0:T(8,128)(2,1)}, u32[]{:S(2)}, u32[]{:S(2)}) collective-permute-start(bf16[1024,512]{1,0:T(8,128)(2,1)} %get-tuple-element.26.refs_10_), channel_id=1, source_target_pairs={{0,24},{8,0},{16,8},{24,16},{1,25},{9,1},{17,9},{25,17},{2,26},{10... | collective-permute-start | bytes 3145736 | tf_op jit(solution)/shard_map/ppermute | solution.py:389
  79.1 19.0 %collective-permute-start.13 = (bf16[512,512]{1,0:T(8,128)(2,1)}, bf16[512,512]{1,0:T(8,128)(2,1)S(1)}, u32[]{:S(2)}, u32[]{:S(2)}) collective-permute-start(bf16[512,512]{1,0:T(8,128)(2,1)} %get-tuple-element.27), channel_id=1, source_target_pairs={{0,2},{2,4},{4,6},{6,0},{1,3},{3,5},{5,7},{7,1},{8,10},{10,12},{12... | collective-permute-start | bytes 1572872 | tf_op jit(solution)/shard_map/ppermute | solution.py:389
  79.1 19.0 %collective-permute-start.14 = (bf16[512,512]{1,0:T(8,128)(2,1)}, bf16[512,512]{1,0:T(8,128)(2,1)S(1)}, u32[]{:S(2)}, u32[]{:S(2)}) collective-permute-start(bf16[512,512]{1,0:T(8,128)(2,1)} %get-tuple-element.28), channel_id=1, source_target_pairs={{0,6},{2,0},{4,2},{6,4},{1,7},{3,1},{5,3},{7,5},{8,14},{10,8},{12,... | collective-permute-start | bytes 1572872 | tf_op jit(solution)/shard_map/ppermute | solution.py:389
  82.4 15.8 %collective-permute-start.15 = (bf16[512,512]{1,0:T(8,128)(2,1)}, bf16[512,512]{1,0:T(8,128)(2,1)S(1)}, u32[]{:S(2)}, u32[]{:S(2)}) collective-permute-start(bf16[512,512]{1,0:T(8,128)(2,1)} %get-tuple-element.29), channel_id=1, source_target_pairs={{0,8},{8,16},{16,24},{24,0},{1,9},{9,17},{17,25},{25,1},{2,10},{10... | collective-permute-start | bytes 1572872 | tf_op jit(solution)/shard_map/ppermute | solution.py:389
  82.4 15.8 %collective-permute-start.16 = (bf16[512,512]{1,0:T(8,128)(2,1)}, bf16[512,512]{1,0:T(8,128)(2,1)S(1)}, u32[]{:S(2)}, u32[]{:S(2)}) collective-permute-start(bf16[512,512]{1,0:T(8,128)(2,1)} %get-tuple-element.30), channel_id=1, source_target_pairs={{0,24},{8,0},{16,8},{24,16},{1,25},{9,1},{17,9},{25,17},{2,26},{10... | collective-permute-start | bytes 1572872 | tf_op jit(solution)/shard_map/ppermute | solution.py:389
  130.6 53.2 %all-to-all-start = ((bf16[64,256,128]{2,1,0:T(8,128)(2,1)}), bf16[64,256,128]{2,1,0:T(8,128)(2,1)}, u32[]{:S(2)}, u32[]{:S(2)}) async-start(bf16[64,256,128]{2,1,0:T(8,128)(2,1)} %shard_map.113), calls=%async_computation | async-start | bytes 8388608 | tf_op jit(solution)/shard_map/all_to_all | solution.py:494
  136.5 79.9 %copy-start = (f32[256,512]{1,0:T(8,128)S(1)}, f32[256,512]{1,0:T(8,128)}, u32[]{:S(2)}) copy-start(f32[256,512]{1,0:T(8,128)} %d_ref.1) | copy-start | bytes 1572868
  136.5 79.9 %copy-start.4 = (f32[256,512]{1,0:T(8,128)S(1)}, f32[256,512]{1,0:T(8,128)}, u32[]{:S(2)}) copy-start(f32[256,512]{1,0:T(8,128)} %r_ref.1) | copy-start | bytes 1572868
  188.7 22.0 %all-to-all-start.1 = ((f32[128,1,128]{2,1,0:T(1,128)}), f32[128,1,128]{2,1,0:T(1,128)S(1)}, u32[]{:S(2)}, u32[]{:S(2)}) async-start(f32[128,1,128]{2,1,0:T(1,128)} %bitcast.43), calls=%async_computation.1 | async-start | bytes 131072 | tf_op jit(solution)/shard_map/all_to_all | solution.py:500
  202.7 12.6 %collective-permute-start.17 = (f32[128,256]{1,0:T(8,128)}, f32[128,256]{1,0:T(8,128)S(1)}, u32[]{:S(2)}, u32[]{:S(2)}) collective-permute-start(f32[128,256]{1,0:T(8,128)} %get-tuple-element.32), channel_id=1, source_target_pairs={{0,32},{32,0},{1,33},{33,1},{2,34},{34,2},{3,35},{35,3},{4,36},{36... | collective-permute-start | bytes 393224 | tf_op jit(solution)/shard_map/ppermute | solution.py:502
  202.9 13.3 %collective-permute-start.19 = (f32[128,256]{1,0:T(8,128)}, f32[128,256]{1,0:T(8,128)S(1)}, u32[]{:S(2)}, u32[]{:S(2)}) collective-permute-start(f32[128,256]{1,0:T(8,128)} %get-tuple-element.32), channel_id=1, source_target_pairs={{0,96},{32,64},{64,32},{96,0},{1,97},{33,65},{65,33},{97,1},{2,98}... | collective-permute-start | bytes 393224 | tf_op jit(solution)/shard_map/ppermute | solution.py:504
  204.1 12.2 %collective-permute-start.18 = (f32[128,256]{1,0:T(8,128)}, f32[128,256]{1,0:T(8,128)S(1)}, u32[]{:S(2)}, u32[]{:S(2)}) collective-permute-start(f32[128,256]{1,0:T(8,128)} %get-tuple-element.32), channel_id=1, source_target_pairs={{0,64},{64,0},{1,65},{65,1},{2,66},{66,2},{3,67},{67,3},{4,68},{68... | collective-permute-start | bytes 393224 | tf_op jit(solution)/shard_map/ppermute | solution.py:503
  (18 other events, 161.0 us)

commit v3 on v2

--- a/solution.py
+++ b/solution.py
@@ -16,8 +16,9 @@
 HALF = 256
 WIDE = 256
 PER = 8
-VMEM = 56 * 1024 * 1024
+VMEM = 16 * 1024 * 1024
 NT = (((1,), (1,)), ((), ()))
+TOKEN = pl.BlockSpec(memory_space=pltpu.SMEM)
 Y_SWAP = [(0, 3), (3, 0), (2, 1), (1, 2)]
 
 
@@ -30,91 +31,77 @@
 Q_STEP = 4
 
 
-def _probs_kernel(off, qa_ref, ka_ref, qb_ref, kb_ref, p0_ref, p1_ref):
+def _probs_kernel(off, q_ref, k_ref, p0_ref, p1_ref, token):
     del off
+    token[0] = 0
     factor = math.log2(math.e) / math.sqrt(HD)
     rows = lax.broadcasted_iota(jnp.int32, (HALF, HALF), 0)
     cols = lax.broadcasted_iota(jnp.int32, (HALF, HALF), 1)
     seen = rows <= cols
 
-    def go(q_ref, k_ref):
-        for j in range(Q_STEP):
-            q = q_ref[:, j * HD : (j + 1) * HD]
-            out = slice(j * HALF, (j + 1) * HALF)
-            diag = lax.dot_general(
-                k_ref[:HALF], q[:HALF], NT, preferred_element_type=F32
-            )
-            diag = jnp.where(seen, diag, -jnp.inf)
-            top = jnp.max(diag, axis=0, keepdims=True)
-            e = jnp.exp2((diag - top) * factor)
-            inv = 1.0 / jnp.sum(e, axis=0, keepdims=True)
-            p0_ref[:, out] = (e * inv).astype(BF)
-            low = lax.dot_general(
-                k_ref[:HALF], q[HALF:], NT, preferred_element_type=F32
-            )
-            diag = lax.dot_general(
-                k_ref[HALF:], q[HALF:], NT, preferred_element_type=F32
-            )
-            diag = jnp.where(seen, diag, -jnp.inf)
-            top = jnp.maximum(
-                jnp.max(low, axis=0, keepdims=True),
-                jnp.max(diag, axis=0, keepdims=True),
-            )
-            e = jnp.exp2((low - top) * factor)
-            f = jnp.exp2((diag - top) * factor)
-            inv = 1.0 / (
-                jnp.sum(e, axis=0, keepdims=True) + jnp.sum(f, axis=0, keepdims=True)
-            )
-            p1_ref[:HALF, out] = (e * inv).astype(BF)
-            p1_ref[HALF:, out] = (f * inv).astype(BF)
-
-    @pl.when(pl.program_id(0) == 0)
-    def _():
-        go(qa_ref, ka_ref)
-
-    @pl.when(pl.program_id(0) == 1)
-    def _():
-        go(qb_ref, kb_ref)
-
-
-def probs_of(core, queries, keys, other):
+    for j in range(Q_STEP):
+        q = q_ref[:, j * HD : (j + 1) * HD]
+        out = slice(j * HALF, (j + 1) * HALF)
+        diag = lax.dot_general(
+            k_ref[:HALF], q[:HALF], NT, preferred_element_type=F32
+        )
+        diag = jnp.where(seen, diag, -jnp.inf)
+        top = jnp.max(diag, axis=0, keepdims=True)
+        e = jnp.exp2((diag - top) * factor)
+        inv = 1.0 / jnp.sum(e, axis=0, keepdims=True)
+        p0_ref[:, out] = (e * inv).astype(BF)
+        low = lax.dot_general(
+            k_ref[:HALF], q[HALF:], NT, preferred_element_type=F32
+        )
+        diag = lax.dot_general(
+            k_ref[HALF:], q[HALF:], NT, preferred_element_type=F32
+        )
+        diag = jnp.where(seen, diag, -jnp.inf)
+        top = jnp.maximum(
+            jnp.max(low, axis=0, keepdims=True),
+            jnp.max(diag, axis=0, keepdims=True),
+        )
+        e = jnp.exp2((low - top) * factor)
+        f = jnp.exp2((diag - top) * factor)
+        inv = 1.0 / (
+            jnp.sum(e, axis=0, keepdims=True) + jnp.sum(f, axis=0, keepdims=True)
+        )
+        p1_ref[:HALF, out] = (e * inv).astype(BF)
+        p1_ref[HALF:, out] = (f * inv).astype(BF)
+
+
+def probs_of(at, queries, keys):
     heads = 2 * PER
     steps = heads // Q_STEP
     per = steps // 2
     wide = Q_STEP * HALF
-
-    def first(s, i):
-        return jnp.where(s == 0, i, steps - 1)
-
     return pl.pallas_call(
         _probs_kernel,
         grid_spec=pltpu.PrefetchScalarGridSpec(
             num_scalar_prefetch=1,
-            grid=(2, steps),
+            grid=(steps,),
             in_specs=[
-                pl.BlockSpec(
-                    (LEN, Q_STEP * HD), lambda s, i, o: (0, o[0] * steps + first(s, i))
-                ),
-                pl.BlockSpec((LEN, HD), lambda s, i, o: (0, o[0] * 2 + first(s, i) // per)),
-                pl.BlockSpec((LEN, Q_STEP * HD), lambda s, i, o: (0, s * i)),
-                pl.BlockSpec((LEN, HD), lambda s, i, o: (0, heads + s * (i // per))),
+                pl.BlockSpec((LEN, Q_STEP * HD), lambda i, o: (0, o[0] + i)),
+                pl.BlockSpec((LEN, HD), lambda i, o: (0, o[1] + i // per)),
             ],
             out_specs=[
-                pl.BlockSpec((HALF, wide), lambda s, i, o: (0, s * steps + i)),
-                pl.BlockSpec((LEN, wide), lambda s, i, o: (0, s * steps + i)),
+                pl.BlockSpec((HALF, wide), lambda i, o: (0, i)),
+                pl.BlockSpec((LEN, wide), lambda i, o: (0, i)),
+                TOKEN,
             ],
         ),
         out_shape=[
-            jax.ShapeDtypeStruct((HALF, 2 * heads * HALF), BF),
-            jax.ShapeDtypeStruct((LEN, 2 * heads * HALF), BF),
+            pltpu.HBM((HALF, heads * HALF), BF),
+            pltpu.HBM((LEN, heads * HALF), BF),
+            jax.ShapeDtypeStruct((1,), jnp.int32),
         ],
-        compiler_params=_params(2),
+        compiler_params=_params(1),
         cost_estimate=pl.CostEstimate(
-            flops=2 * heads * 3 * HALF * HALF * HD * 2,
-            bytes_accessed=2 * heads * (3 * HALF * HALF + LEN * HD) * 2,
-            transcendentals=2 * heads * 3 * HALF * HALF,
-        ),
-    )(core, queries, keys, other, other)
+            flops=heads * 3 * HALF * HALF * HD * 2,
+            bytes_accessed=heads * (3 * HALF * HALF + LEN * HD) * 2,
+            transcendentals=heads * 3 * HALF * HALF,
+        ),
+    )(at, queries, keys)
 
 
 SHARD = 256
@@ -127,6 +114,9 @@
     n = len(counts)
     streams, refs = (refs[:n], refs[n : 2 * n]), refs[2 * n :]
     k = pl.program_id(0)
+    if not last:
+        refs[-1][0] = 0
+        refs = refs[:-1]
     acc = refs[-1]
 
     @pl.when(k == 0)
@@ -189,12 +179,15 @@
             num_scalar_prefetch=1,
             grid=(n,),
             in_specs=[*x_specs, *w_specs, *([] if first else [whole])],
-            out_specs=pl.BlockSpec((2 * WIDE, 2 * LEN), lambda k, w: (0, 0)) if last else whole,
+            out_specs=pl.BlockSpec((2 * WIDE, 2 * LEN), lambda k, w: (0, 0)) if last else [whole, TOKEN],
             scratch_shapes=[pltpu.VMEM((2 * LEN, 2 * WIDE), F32)] if last else [],
         ),
         out_shape=jax.ShapeDtypeStruct((2 * WIDE, 2 * LEN), BF)
         if last
-        else jax.ShapeDtypeStruct((2 * LEN, 2 * WIDE), F32),
+        else [
+            (pltpu.HBM if first else jax.ShapeDtypeStruct)((2 * LEN, 2 * WIDE), F32),
+            jax.ShapeDtypeStruct((1,), jnp.int32),
+        ],
         compiler_params=_params(1),
         cost_estimate=pl.CostEstimate(
             flops=2 * LEN * deep * 2 * n * 2 * WIDE * 2,
@@ -214,14 +207,12 @@
 H_STEP = 4
 
 
-def _pull_kernel(p0_ref, p1_ref, v_ref, t_ref, o_ref, acc):
-    h = pl.program_id(2)
+def _pull_kernel(a0_ref, a1_ref, b0_ref, b1_ref, v_ref, t_ref, o_ref, acc):
+    s, h = pl.program_id(0), pl.program_id(2)
 
     @pl.when(h == 0)
     def _():
         acc[...] = jnp.zeros_like(acc)
-
-    both = jnp.concatenate([v_ref[...], t_ref[...]], axis=0)
 
     def back(o):
         out, tan = o[:HD], o[HD:]
@@ -231,25 +222,44 @@
         pull = inv2 * cross * (1.0 + EPSILON * inv2)
         return (inv2 * (tan - out * pull)).astype(BF)
 
-    w0 = back(jnp.dot(both[:, :HALF], p0_ref[...], preferred_element_type=F32))
-    w1 = back(jnp.dot(both, p1_ref[...], preferred_element_type=F32))
-    acc[:HALF] += lax.dot_general(p0_ref[...], w0, NT, preferred_element_type=F32)
-    acc[...] += lax.dot_general(p1_ref[...], w1, NT, preferred_element_type=F32)
+    def go(p0_ref, p1_ref):
+        both = jnp.concatenate([v_ref[...], t_ref[...]], axis=0)
+        w0 = back(jnp.dot(both[:, :HALF], p0_ref[...], preferred_element_type=F32))
+        w1 = back(jnp.dot(both, p1_ref[...], preferred_element_type=F32))
+        acc[:HALF] += lax.dot_general(p0_ref[...], w0, NT, preferred_element_type=F32)
+        acc[...] += lax.dot_general(p1_ref[...], w1, NT, preferred_element_type=F32)
+
+    @pl.when(s == 0)
+    def _():
+        go(a0_ref, a1_ref)
+
+    @pl.when(s == 1)
+    def _():
+        go(b0_ref, b1_ref)
 
     @pl.when(h == PER // H_STEP - 1)
     def _():
         o_ref[...] = acc[...].T.astype(BF)
 
 
-def pull_back(p0, p1, projected):
+def pull_back(a0, a1, b0, b1, projected):
     steps = PER // H_STEP
     wide = H_STEP * HALF
+
+    def in_a(s, g, h):
+        return 0, jnp.where(s == 0, g * steps + h, 2 * steps - 1)
+
+    def in_b(s, g, h):
+        return 0, s * (g * steps + h)
+
     return pl.pallas_call(
         _pull_kernel,
         grid=(2, 2, steps),
         in_specs=[
-            pl.BlockSpec((HALF, wide), lambda s, g, h: (0, (s * 2 + g) * steps + h)),
-            pl.BlockSpec((LEN, wide), lambda s, g, h: (0, (s * 2 + g) * steps + h)),
+            pl.BlockSpec((HALF, wide), in_a),
+            pl.BlockSpec((LEN, wide), in_a),
+            pl.BlockSpec((HALF, wide), in_b),
+            pl.BlockSpec((LEN, wide), in_b),
             pl.BlockSpec((HD, LEN), lambda s, g, h: (g, s)),
             pl.BlockSpec((HD, LEN), lambda s, g, h: (2 + g, s)),
         ],
@@ -257,7 +267,7 @@
         out_shape=jax.ShapeDtypeStruct((WIDE, 2 * LEN), BF),
         scratch_shapes=[pltpu.VMEM((LEN, HD), F32)],
         compiler_params=_params(3),
-    )(p0, p1, projected, projected)
+    )(a0, a1, b0, b1, projected, projected)
 
 
 G_COLS = 2048
@@ -283,7 +293,7 @@
             pl.BlockSpec((LEN, G_COLS), lambda i: (0, i)),
         ],
         out_specs=pl.BlockSpec((G_COLS // OWN, WIDE, OWN), lambda i: (i, 0, 0)),
-        out_shape=jax.ShapeDtypeStruct((depth // OWN, WIDE, OWN), BF),
+        out_shape=pltpu.HBM((depth // OWN, WIDE, OWN), BF),
         compiler_params=_params(1),
     )(pulled, pulled, xa, xb)
 
@@ -314,9 +324,7 @@
 
 
 def chosen(yh, own, swapped, after):
-    def kernel(yh_ref, own_ref, swapped_ref, _, low_ref, high_ref, zero_ref):
-        zero_ref[0] = 0
-
+    def kernel(yh_ref, own_ref, swapped_ref, _, low_ref, high_ref):
         @pl.when(yh_ref[0] == 0)
         def _():
             low_ref[...] = own_ref[...]
@@ -330,9 +338,8 @@
     return pl.pallas_call(
         kernel,
         in_specs=[pl.BlockSpec(memory_space=pltpu.SMEM), WHOLE, WHOLE, ANY],
-        out_specs=[WHOLE, WHOLE, pl.BlockSpec(memory_space=pltpu.SMEM)],
-        out_shape=[jax.ShapeDtypeStruct(own.shape, BF)] * 2
-        + [jax.ShapeDtypeStruct((1,), jnp.int32)],
+        out_specs=[WHOLE, WHOLE],
+        out_shape=[jax.ShapeDtypeStruct(own.shape, BF)] * 2,
         compiler_params=pltpu.CompilerParams(vmem_limit_bytes=VMEM),
     )(yh, own, swapped, after)
 
@@ -354,19 +361,19 @@
         in_specs=[
             pl.BlockSpec(shape, lambda i, c=c % 2: (i + c * steps, 0)) for c in range(n)
         ]
-        + [ANY] * len(after),
+        + [TOKEN] * len(after),
         out_specs=[pl.BlockSpec(shape, lambda i: (i, 0))] * n,
         out_shape=[jax.ShapeDtypeStruct((half, shape[1]), BF)] * n,
         compiler_params=_params(1),
     )(*arrays, *after)
 
 
-def joined(lists):
+def joined(lists, after):
     flat = sum(lists, [])
 
     def kernel(*refs):
         at = 0
-        for arrays, o in zip(lists, refs[len(flat) :]):
+        for arrays, o in zip(lists, refs[-len(lists) :]):
             row = 0
             for _ in arrays:
                 n = refs[at].shape[0]
@@ -375,14 +382,39 @@
 
     return pl.pallas_call(
         kernel,
-        in_specs=[WHOLE] * len(flat),
+        in_specs=[WHOLE] * len(flat) + [TOKEN] * len(after),
         out_specs=[WHOLE] * len(lists),
         out_shape=[
             jax.ShapeDtypeStruct((sum(a.shape[0] for a in l), l[0].shape[1]), BF)
             for l in lists
         ],
         compiler_params=pltpu.CompilerParams(vmem_limit_bytes=VMEM),
-    )(*flat)
+    )(*flat, *after)
+
+
+def for_partner(other, queries, keys, after):
+    wide = 2 * PER * HD
+
+    def kernel(other_ref, q_ref, k_ref, _, o_ref):
+        del other_ref
+        o_ref[:, :wide] = q_ref[...]
+        o_ref[:, wide:] = k_ref[...]
+
+    return pl.pallas_call(
+        kernel,
+        grid_spec=pltpu.PrefetchScalarGridSpec(
+            num_scalar_prefetch=1,
+            grid=(1,),
+            in_specs=[
+                pl.BlockSpec((LEN, wide), lambda i, o: (0, o[0])),
+                pl.BlockSpec((LEN, WIDE), lambda i, o: (0, o[0])),
+                ANY,
+            ],
+            out_specs=pl.BlockSpec((LEN, wide + WIDE), lambda i, o: (0, 0)),
+        ),
+        out_shape=jax.ShapeDtypeStruct((LEN, wide + WIDE), BF),
+        compiler_params=_params(1),
+    )(other, queries, keys, after)
 
 
 def hop(x, axis, by):
@@ -457,25 +489,18 @@
     x, z, yh = (lax.axis_index(a) for a in ("x", "z", "yh"))
     other = 1 - core
     swap = [(0, 1), (1, 0)]
-    heads = 2 * PER * HD
-
-    def cols(a, which, width):
-        return lax.dynamic_slice_in_dim(a, which * width, width, 1)
 
     own = narrow(core[None], value_weight, direction)
     normed_b = lax.ppermute(normed, "c", swap)
     swapped = lax.ppermute(own, ("yl", "yh"), Y_SWAP)
-    *near, _ = chosen(yh[None], own, swapped, own)
-    *far, zero = chosen(yh[None], own, swapped, normed_b)
-    later = other + zero[0]
-    partner = jnp.concatenate([cols(queries, later, heads), cols(keys, later, WIDE)], 1)
-    partner = lax.ppermute(partner, "c", swap)
     inner = [
-        [a, hop(a, axis, 1), hop(a, axis, 3), hop(b, axis, 2)]
-        for a, b, axis in zip(near, far, "xz")
+        [a, *(hop(a, axis, by) for by in (1, 3, 2))]
+        for a, axis in zip(chosen(yh[None], own, swapped, normed_b), "xz")
     ]
-    lines = joined(inner)
-    p0, p1 = probs_of(core[None], queries, keys, partner)
+    *probs_a, done_a = probs_of(jnp.stack([core * 4, core * 2]), queries, keys)
+    lines = joined(inner, [done_a])
+    partner = lax.ppermute(for_partner(other[None], queries, keys, lines[0]), "c", swap)
+    *probs_b, done_b = probs_of(jnp.array([0, 2 * PER], jnp.int32), partner, partner)
     turn = (0, -1, 1, 2)
 
     def places(steps):
@@ -483,13 +508,14 @@
         b_at = [((x + s) % 4) * 8 + (z + i) % 4 * 2 + 1 for s in steps for i in turn]
         return jnp.stack(a_at + b_at).astype(jnp.int32)
 
-    some = project(places((0,)), normed, normed_b, lines[:1], lines[1:])
-    (_, *a, a_far, a_far2), (_, *b, b_far, b_far2) = rings(lines, "zx", [p0, some])
-    most = project(places((-1, 1)), normed, normed_b, a, b, some)
+    held = pltpu.with_memory_space_constraint(normed, pltpu.HBM)
+    some, done_some = project(places((0,)), held, normed_b, lines[:1], lines[1:])
+    (_, *a, a_far, a_far2), (_, *b, b_far, b_far2) = rings(lines, "zx", [done_b, done_some])
+    most, _ = project(places((-1, 1)), held, normed_b, a, b, some)
     projected = project(
-        places((2,)), normed, normed_b, [a_far, a_far2], [b_far, b_far2], most, True
+        places((2,)), held, normed_b, [a_far, a_far2], [b_far, b_far2], most, True
     )
-    pulled = pull_back(p0, p1, projected)
+    pulled = pull_back(*probs_a, *probs_b, projected)
     parts = curvature(pulled, normed, normed_b)
     parts = lax.all_to_all(parts, CHIPS, 0, 0, tiled=True)
     everyone = ("c",) + CHIPS

time: 221 us -> 207 us (0.937)
  Pallas kernels: 77.6 us -> 67.4 us
  waiting for transfers between devices: 72.1 us -> 78.6 us
  starting transfers between devices: 49 us -> 43.7 us
  other arithmetic: 4.67 us -> 1.69 us
    pallas_call x3, Pallas kernels: 26 us -> 21.7 us  [project(): pl.pallas_call(kernel, grid_spec=pltpu.PrefetchScalarGridSpec(num_scalar_...]
    all_to_all x1, starting transfers between devices: 14.1 us -> 9.86 us  [body(): rows = lax.all_to_all(rows, everyone, 0, 0, tiled=True)]
    ppermute x14, waiting for transfers between devices: 9.14 us -> 13 us  [hop(): return lax.ppermute(x, axis, [(i, (i + by) % 4) for i in range(4)])]
    pallas_call x2 -> x1, Pallas kernels: 3.8 us -> 0.03 us  [chosen(): pl.pallas_call(kernel, in_specs=[pl.BlockSpec(memory_space=pltpu.SMEM), W...]
    ppermute x14, starting transfers between devices: 26.2 us -> 23 us  [hop(): return lax.ppermute(x, axis, [(i, (i + by) % 4) for i in range(4)])]
    all_to_all x1, waiting for transfers between devices: 46 us -> 48.7 us  [body(): parts = lax.all_to_all(parts, CHIPS, 0, 0, tiled=True)]
    all_to_all x1, starting transfers between devices: 5.82 us -> 8.25 us  [body(): parts = lax.all_to_all(parts, CHIPS, 0, 0, tiled=True)]
    unnamed x40 -> x30, local copies, waits for them, and re-layouts: 3.71 us -> 6.01 us
  transfers between devices with their start and end apart: 22 -> 22, of which waited for: 8 -> 9; matrix products, arithmetic and copies ran while one was open for 2% -> 1% of each run, Pallas kernels for 17% -> 15%
where the time goes in v3:
time: 207 us; the launch traced here: 203 us
  waiting for transfers between devices  78.6 us (38%)
  Pallas kernels  67.4 us (33%)
  starting transfers between devices  43.7 us (21%)
  local copies, waits for them, and re-layouts  6.86 us (3%)
  between operations  5.31 us (3%)
    all_to_all x1, waiting for transfers between devices, body(): parts = lax.all_to_all(parts, CHIPS, 0, 0, tiled=True)  48.7 us
    ppermute x14, starting transfers between devices, hop(): return lax.ppermute(x, axis, [(i, (i + by) % 4) for i in range(4)])  23 us
    pallas_call x3, Pallas kernels, project(): pl.pallas_call(kernel, grid_spec=pltpu.PrefetchScalarGridSpec(num_scalar_...  21.7 us
    pallas_call x2, Pallas kernels, probs_of(): pl.pallas_call(_probs_kernel, grid_spec=pltpu.PrefetchScalarGridSpec(num_...  14.7 us
    ppermute x14, waiting for transfers between devices, hop(): return lax.ppermute(x, axis, [(i, (i + by) % 4) for i in range(4)])  13 us
    pallas_call x1, Pallas kernels, pull_back(): pl.pallas_call(_pull_kernel, grid=(2, 2, steps), in_specs=[pl.BlockSpec((...  10.4 us
    all_to_all x1, starting transfers between devices, body(): rows = lax.all_to_all(rows, everyone, 0, 0, tiled=True)  9.86 us
    pallas_call x1, Pallas kernels, curvature(): pl.pallas_call(_ggn_kernel, grid=(depth // G_COLS,), in_specs=[pl.BlockSp...  8.78 us
  transfers between devices with their start and end apart: 22, of which 9 were waited for; matrix products, arithmetic and copies ran while one was open for 1% of the time, Pallas kernels for 15%

profile of v3, /device:TPU:16, one launch (start us, length us, event | category | flops | bytes accessed | tf_op | source)
XLA Modules:
  0.0 203.5 jit_solution(14349626427895606987)
XLA Ops:
  3.3 8.2 %collective-permute-done.swapped_ref = bf16[256,512]{1,0:T(8,128)(2,1)S(1)} collective-permute-done((bf16[256,512]{1,0:T(8,128)(2,1)S(1)}, bf16[256,512]{1,0:T(8,128)(2,1)S(1)}, u32[]{:S(2)}, u32[]{:S(2)}) %collective-permute-start) | collective-permute-done | bytes 262176 | tf_op jit(solution)/shard_map/ppermute | solution.py:495
  11.5 2.7 %collective-permute-done.1._.refs_5_.refs_6_.refs_7_.refs_8_.xb_ref = bf16[512,8192]{1,0:T(8,128)(2,1)} collective-permute-done((bf16[512,8192]{1,0:T(8,128)(2,1)}, bf16[512,8192]{1,0:T(8,128)(2,1)}, u32[]{:S(2)}, u32[]{:S(2)}) %collective-permute-start.1) | collective-permute-done | bytes 8388640 | tf_op jit(solution)/shard_map/ppermute | solution.py:494
  14.3 3.1 %collective-permute-start.4 = (bf16[256,512]{1,0:T(8,128)(2,1)S(1)}, bf16[256,512]{1,0:T(8,128)(2,1)S(1)}, u32[]{:S(2)}, u32[]{:S(2)}) collective-permute-start(bf16[256,512]{1,0:T(8,128)(2,1)S(1)} %get-tuple-element.24.refs_0_), channel_id=1, source_target_pairs={{0,16},{8,24},{16,0},{24,8},{1,17},{9,25},{17,1},{25,9},{2,18},{10... | collective-permute-start | bytes 786440 | tf_op jit(solution)/shard_map/ppermute | solution.py:421
  19.4 3.9 %collective-permute-start.7 = (bf16[256,512]{1,0:T(8,128)(2,1)S(1)}, bf16[256,512]{1,0:T(8,128)(2,1)S(1)}, u32[]{:S(2)}, u32[]{:S(2)}) collective-permute-start(bf16[256,512]{1,0:T(8,128)(2,1)S(1)} %get-tuple-element.25.refs_4_), channel_id=1, source_target_pairs={{0,4},{2,6},{4,0},{6,2},{1,5},{3,7},{5,1},{7,3},{8,12},{10,14},{12... | collective-permute-start | bytes 786440 | tf_op jit(solution)/shard_map/ppermute | solution.py:421
  27.0 2.2 %copy-done.2 = bf16[512,4096]{1,0:T(8,128)(2,1)S(1)} copy-done((bf16[512,4096]{1,0:T(8,128)(2,1)S(1)}, bf16[512,4096]{1,0:T(8,128)(2,1)}, u32[]{:S(2)}) %copy-start.2) | copy-done | bytes 4194328
  29.2 6.8 %shard_map.112 = (bf16[256,4096]{1,0:T(8,128)(2,1)}, bf16[512,4096]{1,0:T(8,128)(2,1)}, s32[1]{0:T(128)}) custom-call(s32[2]{0:T(128)S(1)} %pad_add_fusion.1.off, bf16[512,4096]{1,0:T(8,128)(2,1)S(1)} %copy-done.2, bf16[512,512]{1,0:T(8,128)(2,1)S(1)} %copy-done.10), custom_call_target="tpu_custom_call" | custom-call | flops 805306368 | bytes 8388608 | tf_op jit(solution)/shard_map/pallas_call | solution.py:78
  39.6 2.8 %collective-permute-start.12 = (bf16[1024,512]{1,0:T(8,128)(2,1)}, bf16[1024,512]{1,0:T(8,128)(2,1)S(1)}, u32[]{:S(2)}, u32[]{:S(2)}) collective-permute-start(bf16[1024,512]{1,0:T(8,128)(2,1)} %get-tuple-element.30.refs_10_), channel_id=1, source_target_pairs={{0,24},{8,0},{16,8},{24,16},{1,25},{9,1},{17,9},{25,17},{2,26},{10... | collective-permute-start | bytes 3145736 | tf_op jit(solution)/shard_map/ppermute | solution.py:421
  42.4 2.1 %collective-permute-start.10 = (bf16[1024,512]{1,0:T(8,128)(2,1)}, bf16[1024,512]{1,0:T(8,128)(2,1)S(1)}, u32[]{:S(2)}, u32[]{:S(2)}) collective-permute-start(bf16[1024,512]{1,0:T(8,128)(2,1)} %get-tuple-element.27._.refs_9_), channel_id=1, source_target_pairs={{0,6},{2,0},{4,2},{6,4},{1,7},{3,1},{5,3},{7,5},{8,14},{10,8},{12,... | collective-permute-start | bytes 3145736 | tf_op jit(solution)/shard_map/ppermute | solution.py:421
  44.6 6.8 %shard_map.118 = (f32[1024,512]{1,0:T(8,128)}, s32[1]{0:T(128)}) custom-call(s32[8]{0:T(128)S(1)} %stack.146.refs_0_, bf16[512,8192]{1,0:T(8,128)(2,1)} %xa_ref.1, bf16[512,8192]{1,0:T(8,128)(2,1)} %xa_ref.1, bf16[512,8192]{1,0:T(8,128)(2,1)} %xa_ref.1, bf16[512,8192]{1,0:T(8,128)(2,1)} %xa_ref.1, ...), custom_call_target="tpu_custom_call" | custom-call | flops 2147483648 | bytes 6291456 | tf_op jit(solution)/shard_map/pallas_call | solution.py:176
  51.4 7.9 %shard_map.117 = (bf16[256,4096]{1,0:T(8,128)(2,1)}, bf16[512,4096]{1,0:T(8,128)(2,1)}, s32[1]{0:T(128)}) custom-call(s32[2]{0:T(128)S(1)} %iota_multiply_fusion.off, bf16[512,2304]{1,0:T(8,128)(2,1)} %collective-permute-done.8.q_ref.k_ref, bf16[512,2304]{1,0:T(8,128)(2,1)} %collective-permute-done.8.q_ref.k_ref), custom_call_target="tpu_custom_call" | custom-call | flops 805306368 | bytes 8388608 | tf_op jit(solution)/shard_map/pallas_call | solution.py:78
  59.3 6.5 %collective-permute-done.12.refs_3_.refs_12_ = bf16[1024,512]{1,0:T(8,128)(2,1)S(1)} collective-permute-done((bf16[1024,512]{1,0:T(8,128)(2,1)}, bf16[1024,512]{1,0:T(8,128)(2,1)S(1)}, u32[]{:S(2)}, u32[]{:S(2)}) %collective-permute-start.12) | collective-permute-done | bytes 1048608 | tf_op jit(solution)/shard_map/ppermute | solution.py:421
  65.8 3.3 %collective-permute-done.11.refs_2_.refs_11_ = bf16[1024,512]{1,0:T(8,128)(2,1)S(1)} collective-permute-done((bf16[1024,512]{1,0:T(8,128)(2,1)}, bf16[1024,512]{1,0:T(8,128)(2,1)S(1)}, u32[]{:S(2)}, u32[]{:S(2)}) %collective-permute-start.11) | collective-permute-done | bytes 1048608 | tf_op jit(solution)/shard_map/ppermute | solution.py:421
  71.1 3.5 %shard_map.119 = (bf16[512,512]{1,0:T(8,128)(2,1)}, bf16[512,512]{1,0:T(8,128)(2,1)}, bf16[512,512]{1,0:T(8,128)(2,1)}, bf16[512,512]{1,0:T(8,128)(2,1)}) custom-call(bf16[1024,512]{1,0:T(8,128)(2,1)} %collective-permute-done.9.refs_0_.refs_9_, bf16[1024,512]{1,0:T(8,128)(2,1)S(1)} %collective-permute-done.10.refs_1_.refs_10_, ...), custom_call_target="tpu_custom_call" | custom-call | tf_op jit(solution)/shard_map/pallas_call | solution.py:358
  74.6 3.2 %collective-permute-start.14 = (bf16[512,512]{1,0:T(8,128)(2,1)}, bf16[512,512]{1,0:T(8,128)(2,1)}, u32[]{:S(2)}, u32[]{:S(2)}) collective-permute-start(bf16[512,512]{1,0:T(8,128)(2,1)} %get-tuple-element.34), channel_id=1, source_target_pairs={{0,6},{2,0},{4,2},{6,4},{1,7},{3,1},{5,3},{7,5},{8,14},{10,8},{12,... | collective-permute-start | bytes 1572872 | tf_op jit(solution)/shard_map/ppermute | solution.py:421
  78.3 2.8 %collective-permute-start.16 = (bf16[512,512]{1,0:T(8,128)(2,1)}, bf16[512,512]{1,0:T(8,128)(2,1)}, u32[]{:S(2)}, u32[]{:S(2)}) collective-permute-start(bf16[512,512]{1,0:T(8,128)(2,1)} %get-tuple-element.36), channel_id=1, source_target_pairs={{0,24},{8,0},{16,8},{24,16},{1,25},{9,1},{17,9},{25,17},{2,26},{10... | collective-permute-start | bytes 1572872 | tf_op jit(solution)/shard_map/ppermute | solution.py:421
  82.8 8.6 %shard_map.120 = (f32[1024,512]{1,0:T(8,128)S(1)}, s32[1]{0:T(128)}) custom-call(s32[16]{0:T(128)S(1)} %stack.163.refs_0_, bf16[512,8192]{1,0:T(8,128)(2,1)} %xa_ref.1, bf16[512,8192]{1,0:T(8,128)(2,1)} %xa_ref.1, bf16[512,8192]{1,0:T(8,128)(2,1)} %xa_ref.1, bf16[512,8192]{1,0:T(8,128)(2,1)} %xa_ref.1, ...), custom_call_target="tpu_custom_call" | custom-call | flops 4294967296 | bytes 12582912 | tf_op jit(solution)/shard_map/pallas_call | solution.py:176
  91.7 6.3 %shard_map.121.v_ref.t_ref = bf16[512,1024]{1,0:T(8,128)(2,1)S(1)} custom-call(s32[8]{0:T(128)S(1)} %stack.137.refs_0_, bf16[512,8192]{1,0:T(8,128)(2,1)} %xa_ref.1, bf16[512,8192]{1,0:T(8,128)(2,1)} %xa_ref.1, bf16[512,8192]{1,0:T(8,128)(2,1)} %xa_ref.1, bf16[512,8192]{1,0:T(8,128)(2,1)} %xa_ref.1, ...), custom_call_target="tpu_custom_call" | custom-call | flops 2147483648 | bytes 6291456 | tf_op jit(solution)/shard_map/pallas_call | solution.py:176
  98.3 10.4 %shard_map.122.pa_ref.pb_ref = bf16[256,1024]{1,0:T(8,128)(2,1)S(1)} custom-call(bf16[256,4096]{1,0:T(8,128)(2,1)S(1)} %copy-done.8, bf16[512,4096]{1,0:T(8,128)(2,1)S(1)} %copy-done.4, bf16[256,4096]{1,0:T(8,128)(2,1)S(1)} %copy-done.9, bf16[512,4096]{1,0:T(8,128)(2,1)S(1)} %copy-done.5, bf16[512,1024]{1,0:T(8,128)(2,1)S(1)} %shard_map.121.v_ref.t_ref, ...), custom_call_target="tpu_custom_call" | custom-call | tf_op jit(solution)/shard_map/pallas_call | solution.py:255
  108.8 8.8 %shard_map.123 = bf16[64,256,128]{2,1,0:T(8,128)(2,1)} custom-call(bf16[256,1024]{1,0:T(8,128)(2,1)S(1)} %shard_map.122.pa_ref.pb_ref, bf16[256,1024]{1,0:T(8,128)(2,1)S(1)} %shard_map.122.pa_ref.pb_ref, bf16[512,8192]{1,0:T(8,128)(2,1)S(1)} %bitcast.46, bf16[512,8192]{1,0:T(8,128)(2,1)} %collective-permute-done.1._.refs_5_.refs_6_.refs_7_.refs_8_.xb_ref), custom_call_target="tpu_custom_call" | custom-call | tf_op jit(solution)/shard_map/pallas_call | solution.py:286
  117.5 8.2 %all-to-all-start = ((bf16[64,256,128]{2,1,0:T(8,128)(2,1)}), bf16[64,256,128]{2,1,0:T(8,128)(2,1)}, u32[]{:S(2)}, u32[]{:S(2)}) async-start(bf16[64,256,128]{2,1,0:T(8,128)(2,1)} %shard_map.123), calls=%async_computation | async-start | bytes 8388608 | tf_op jit(solution)/shard_map/all_to_all | solution.py:520
  126.6 48.7 %all-to-all-done.parts_ref = bf16[64,256,128]{2,1,0:T(8,128)(2,1)} async-done(((bf16[64,256,128]{2,1,0:T(8,128)(2,1)}), bf16[64,256,128]{2,1,0:T(8,128)(2,1)}, u32[]{:S(2)}, u32[]{:S(2)}) %all-to-all-start) | async-done | bytes 4194336 | tf_op jit(solution)/shard_map/all_to_all | solution.py:520
  175.3 4.6 %shard_map.124 = (f32[128,256]{1,0:T(8,128)S(1)}, f32[128,128]{1,0:T(8,128)}) custom-call(s32[2]{0:T(128)S(1)} %pad_add_fusion.at_ref, f32[1]{0:T(128)S(6)} %copy.13.damping_ref, bf16[64,256,128]{2,1,0:T(8,128)(2,1)} %all-to-all-done.parts_ref, f32[256,512]{1,0:T(8,128)S(1)} %copy-done.1, f32[256,512]{1,0:T(8,128)S(1)} %copy-done.7), custom_call_target="tpu_custom_call" | custom-call | tf_op jit(solution)/shard_map/pallas_call | solution.py:459
  179.9 9.9 %all-to-all-start.1 = ((f32[128,1,128]{2,1,0:T(1,128)}), f32[128,1,128]{2,1,0:T(1,128)S(1)}, u32[]{:S(2)}, u32[]{:S(2)}) async-start(f32[128,1,128]{2,1,0:T(1,128)} %bitcast.39), calls=%async_computation.1 | async-start | bytes 131072 | tf_op jit(solution)/shard_map/all_to_all | solution.py:526
  191.7 6.0 %all-to-all-done.1 = f32[128,1,128]{2,1,0:T(1,128)S(1)} async-done(((f32[128,1,128]{2,1,0:T(1,128)}), f32[128,1,128]{2,1,0:T(1,128)S(1)}, u32[]{:S(2)}, u32[]{:S(2)}) %all-to-all-start.1) | async-done | bytes 65568 | tf_op jit(solution)/shard_map/all_to_all | solution.py:526
  (75 shorter events, 21.0 us)
Async XLA Ops:
  0.6 13.6 %collective-permute-start.1 = (bf16[512,8192]{1,0:T(8,128)(2,1)}, bf16[512,8192]{1,0:T(8,128)(2,1)}, u32[]{:S(2)}, u32[]{:S(2)}) collective-permute-start(bf16[512,8192]{1,0:T(8,128)(2,1)} %xa_ref.1), channel_id=1, source_target_pairs={{0,32},{32,0},{1,33},{33,1},{2,34},{34,2},{3,35},{35,3},{4,36},{36... | collective-permute-start | bytes 25165832 | tf_op jit(solution)/shard_map/ppermute | solution.py:494
  2.8 8.8 %collective-permute-start = (bf16[256,512]{1,0:T(8,128)(2,1)S(1)}, bf16[256,512]{1,0:T(8,128)(2,1)S(1)}, u32[]{:S(2)}, u32[]{:S(2)}) collective-permute-start(bf16[256,512]{1,0:T(8,128)(2,1)S(1)} %shard_map.113.own_ref), channel_id=1, source_target_pairs={{0,65},{65,0},{64,1},{1,64},{2,67},{67,2},{66,3},{3,66},{4,69},{69... | collective-permute-start | bytes 786440 | tf_op jit(solution)/shard_map/ppermute | solution.py:495
  14.3 10.7 %collective-permute-start.4 = (bf16[256,512]{1,0:T(8,128)(2,1)S(1)}, bf16[256,512]{1,0:T(8,128)(2,1)S(1)}, u32[]{:S(2)}, u32[]{:S(2)}) collective-permute-start(bf16[256,512]{1,0:T(8,128)(2,1)S(1)} %get-tuple-element.24.refs_0_), channel_id=1, source_target_pairs={{0,16},{8,24},{16,0},{24,8},{1,17},{9,25},{17,1},{25,9},{2,18},{10... | collective-permute-start | bytes 786440 | tf_op jit(solution)/shard_map/ppermute | solution.py:421
  17.4 18.6 %collective-permute-start.3 = (bf16[256,512]{1,0:T(8,128)(2,1)S(1)}, bf16[256,512]{1,0:T(8,128)(2,1)S(1)}, u32[]{:S(2)}, u32[]{:S(2)}) collective-permute-start(bf16[256,512]{1,0:T(8,128)(2,1)S(1)} %get-tuple-element.24.refs_0_), channel_id=1, source_target_pairs={{0,24},{8,0},{16,8},{24,16},{1,25},{9,1},{17,9},{25,17},{2,26},{10... | collective-permute-start | bytes 786440 | tf_op jit(solution)/shard_map/ppermute | solution.py:421
  18.5 17.4 %collective-permute-start.2 = (bf16[256,512]{1,0:T(8,128)(2,1)S(1)}, bf16[256,512]{1,0:T(8,128)(2,1)S(1)}, u32[]{:S(2)}, u32[]{:S(2)}) collective-permute-start(bf16[256,512]{1,0:T(8,128)(2,1)S(1)} %get-tuple-element.24.refs_0_), channel_id=1, source_target_pairs={{0,8},{8,16},{16,24},{24,0},{1,9},{9,17},{17,25},{25,1},{2,10},{10... | collective-permute-start | bytes 786440 | tf_op jit(solution)/shard_map/ppermute | solution.py:421
  19.4 16.6 %collective-permute-start.7 = (bf16[256,512]{1,0:T(8,128)(2,1)S(1)}, bf16[256,512]{1,0:T(8,128)(2,1)S(1)}, u32[]{:S(2)}, u32[]{:S(2)}) collective-permute-start(bf16[256,512]{1,0:T(8,128)(2,1)S(1)} %get-tuple-element.25.refs_4_), channel_id=1, source_target_pairs={{0,4},{2,6},{4,0},{6,2},{1,5},{3,7},{5,1},{7,3},{8,12},{10,14},{12... | collective-permute-start | bytes 786440 | tf_op jit(solution)/shard_map/ppermute | solution.py:421
  23.3 12.7 %collective-permute-start.6 = (bf16[256,512]{1,0:T(8,128)(2,1)S(1)}, bf16[256,512]{1,0:T(8,128)(2,1)S(1)}, u32[]{:S(2)}, u32[]{:S(2)}) collective-permute-start(bf16[256,512]{1,0:T(8,128)(2,1)S(1)} %get-tuple-element.25.refs_4_), channel_id=1, source_target_pairs={{0,6},{2,0},{4,2},{6,4},{1,7},{3,1},{5,3},{7,5},{8,14},{10,8},{12,... | collective-permute-start | bytes 786440 | tf_op jit(solution)/shard_map/ppermute | solution.py:421
  25.0 11.0 %collective-permute-start.5 = (bf16[256,512]{1,0:T(8,128)(2,1)S(1)}, bf16[256,512]{1,0:T(8,128)(2,1)S(1)}, u32[]{:S(2)}, u32[]{:S(2)}) collective-permute-start(bf16[256,512]{1,0:T(8,128)(2,1)S(1)} %get-tuple-element.25.refs_4_), channel_id=1, source_target_pairs={{0,2},{2,4},{4,6},{6,0},{1,3},{3,5},{5,7},{7,1},{8,10},{10,12},{12... | collective-permute-start | bytes 786440 | tf_op jit(solution)/shard_map/ppermute | solution.py:421
  39.6 11.8 %collective-permute-start.8 = (bf16[512,2304]{1,0:T(8,128)(2,1)}, bf16[512,2304]{1,0:T(8,128)(2,1)}, u32[]{:S(2)}, u32[]{:S(2)}) collective-permute-start(bf16[512,2304]{1,0:T(8,128)(2,1)} %shard_map.116), channel_id=1, source_target_pairs={{0,32},{32,0},{1,33},{33,1},{2,34},{34,2},{3,35},{35,3},{4,36},{36... | collective-permute-start | bytes 7077896 | tf_op jit(solution)/shard_map/ppermute | solution.py:502
  39.6 26.2 %collective-permute-start.12 = (bf16[1024,512]{1,0:T(8,128)(2,1)}, bf16[1024,512]{1,0:T(8,128)(2,1)S(1)}, u32[]{:S(2)}, u32[]{:S(2)}) collective-permute-start(bf16[1024,512]{1,0:T(8,128)(2,1)} %get-tuple-element.30.refs_10_), channel_id=1, source_target_pairs={{0,24},{8,0},{16,8},{24,16},{1,25},{9,1},{17,9},{25,17},{2,26},{10... | collective-permute-start | bytes 3145736 | tf_op jit(solution)/shard_map/ppermute | solution.py:421
  42.4 26.7 %collective-permute-start.11 = (bf16[1024,512]{1,0:T(8,128)(2,1)}, bf16[1024,512]{1,0:T(8,128)(2,1)S(1)}, u32[]{:S(2)}, u32[]{:S(2)}) collective-permute-start(bf16[1024,512]{1,0:T(8,128)(2,1)} %get-tuple-element.30.refs_10_), channel_id=1, source_target_pairs={{0,8},{8,16},{16,24},{24,0},{1,9},{9,17},{17,25},{25,1},{2,10},{10... | collective-permute-start | bytes 3145736 | tf_op jit(solution)/shard_map/ppermute | solution.py:421
  42.4 26.7 %collective-permute-start.10 = (bf16[1024,512]{1,0:T(8,128)(2,1)}, bf16[1024,512]{1,0:T(8,128)(2,1)S(1)}, u32[]{:S(2)}, u32[]{:S(2)}) collective-permute-start(bf16[1024,512]{1,0:T(8,128)(2,1)} %get-tuple-element.27._.refs_9_), channel_id=1, source_target_pairs={{0,6},{2,0},{4,2},{6,4},{1,7},{3,1},{5,3},{7,5},{8,14},{10,8},{12,... | collective-permute-start | bytes 3145736 | tf_op jit(solution)/shard_map/ppermute | solution.py:421
  44.5 26.5 %collective-permute-start.9 = (bf16[1024,512]{1,0:T(8,128)(2,1)}, bf16[1024,512]{1,0:T(8,128)(2,1)}, u32[]{:S(2)}, u32[]{:S(2)}) collective-permute-start(bf16[1024,512]{1,0:T(8,128)(2,1)} %get-tuple-element.27._.refs_9_), channel_id=1, source_target_pairs={{0,2},{2,4},{4,6},{6,0},{1,3},{3,5},{5,7},{7,1},{8,10},{10,12},{12... | collective-permute-start | bytes 3145736 | tf_op jit(solution)/shard_map/ppermute | solution.py:421
  74.6 16.9 %collective-permute-start.13 = (bf16[512,512]{1,0:T(8,128)(2,1)}, bf16[512,512]{1,0:T(8,128)(2,1)}, u32[]{:S(2)}, u32[]{:S(2)}) collective-permute-start(bf16[512,512]{1,0:T(8,128)(2,1)} %get-tuple-element.33), channel_id=1, source_target_pairs={{0,2},{2,4},{4,6},{6,0},{1,3},{3,5},{5,7},{7,1},{8,10},{10,12},{12... | collective-permute-start | bytes 1572872 | tf_op jit(solution)/shard_map/ppermute | solution.py:421
  74.6 16.9 %collective-permute-start.14 = (bf16[512,512]{1,0:T(8,128)(2,1)}, bf16[512,512]{1,0:T(8,128)(2,1)}, u32[]{:S(2)}, u32[]{:S(2)}) collective-permute-start(bf16[512,512]{1,0:T(8,128)(2,1)} %get-tuple-element.34), channel_id=1, source_target_pairs={{0,6},{2,0},{4,2},{6,4},{1,7},{3,1},{5,3},{7,5},{8,14},{10,8},{12,... | collective-permute-start | bytes 1572872 | tf_op jit(solution)/shard_map/ppermute | solution.py:421
  77.8 13.9 %collective-permute-start.15 = (bf16[512,512]{1,0:T(8,128)(2,1)}, bf16[512,512]{1,0:T(8,128)(2,1)}, u32[]{:S(2)}, u32[]{:S(2)}) collective-permute-start(bf16[512,512]{1,0:T(8,128)(2,1)} %get-tuple-element.35), channel_id=1, source_target_pairs={{0,8},{8,16},{16,24},{24,0},{1,9},{9,17},{17,25},{25,1},{2,10},{10... | collective-permute-start | bytes 1572872 | tf_op jit(solution)/shard_map/ppermute | solution.py:421
  78.3 13.4 %collective-permute-start.16 = (bf16[512,512]{1,0:T(8,128)(2,1)}, bf16[512,512]{1,0:T(8,128)(2,1)}, u32[]{:S(2)}, u32[]{:S(2)}) collective-permute-start(bf16[512,512]{1,0:T(8,128)(2,1)} %get-tuple-element.36), channel_id=1, source_target_pairs={{0,24},{8,0},{16,8},{24,16},{1,25},{9,1},{17,9},{25,17},{2,26},{10... | collective-permute-start | bytes 1572872 | tf_op jit(solution)/shard_map/ppermute | solution.py:421
  117.5 57.8 %copy-start.7 = (f32[256,512]{1,0:T(8,128)S(1)}, f32[256,512]{1,0:T(8,128)}, u32[]{:S(2)}) copy-start(f32[256,512]{1,0:T(8,128)} %r_ref.1) | copy-start | bytes 1572868
  117.5 57.7 %all-to-all-start = ((bf16[64,256,128]{2,1,0:T(8,128)(2,1)}), bf16[64,256,128]{2,1,0:T(8,128)(2,1)}, u32[]{:S(2)}, u32[]{:S(2)}) async-start(bf16[64,256,128]{2,1,0:T(8,128)(2,1)} %shard_map.123), calls=%async_computation | async-start | bytes 8388608 | tf_op jit(solution)/shard_map/all_to_all | solution.py:520
  125.8 76.3 %copy-start.12 = (f32[256,512]{1,0:T(8,128)S(1)}, f32[256,512]{1,0:T(8,128)}, u32[]{:S(2)}) copy-start(f32[256,512]{1,0:T(8,128)} %param.13) | copy-start | bytes 1572868
  179.9 17.8 %all-to-all-start.1 = ((f32[128,1,128]{2,1,0:T(1,128)}), f32[128,1,128]{2,1,0:T(1,128)S(1)}, u32[]{:S(2)}, u32[]{:S(2)}) async-start(f32[128,1,128]{2,1,0:T(1,128)} %bitcast.39), calls=%async_computation.1 | async-start | bytes 131072 | tf_op jit(solution)/shard_map/all_to_all | solution.py:526
  189.7 12.3 %collective-permute-start.17 = (f32[128,256]{1,0:T(8,128)S(1)}, f32[128,256]{1,0:T(8,128)S(1)}, u32[]{:S(2)}, u32[]{:S(2)}) collective-permute-start(f32[128,256]{1,0:T(8,128)S(1)} %get-tuple-element.40), channel_id=1, source_target_pairs={{0,32},{32,0},{1,33},{33,1},{2,34},{34,2},{3,35},{35,3},{4,36},{36... | collective-permute-start | bytes 393224 | tf_op jit(solution)/shard_map/ppermute | solution.py:528
  190.0 12.1 %collective-permute-start.18 = (f32[128,256]{1,0:T(8,128)S(1)}, f32[128,256]{1,0:T(8,128)S(1)}, u32[]{:S(2)}, u32[]{:S(2)}) collective-permute-start(f32[128,256]{1,0:T(8,128)S(1)} %get-tuple-element.40), channel_id=1, source_target_pairs={{0,64},{64,0},{1,65},{65,1},{2,66},{66,2},{3,67},{67,3},{4,68},{68... | collective-permute-start | bytes 393224 | tf_op jit(solution)/shard_map/ppermute | solution.py:529
  191.2 10.9 %collective-permute-start.19 = (f32[128,256]{1,0:T(8,128)S(1)}, f32[128,256]{1,0:T(8,128)S(1)}, u32[]{:S(2)}, u32[]{:S(2)}) collective-permute-start(f32[128,256]{1,0:T(8,128)S(1)} %get-tuple-element.40), channel_id=1, source_target_pairs={{0,96},{32,64},{64,32},{96,0},{1,97},{33,65},{65,33},{97,1},{2,98}... | collective-permute-start | bytes 393224 | tf_op jit(solution)/shard_map/ppermute | solution.py:530
  (13 other events, 132.0 us)

commit v4 on v3

--- a/solution.py
+++ b/solution.py
@@ -408,7 +408,7 @@
             in_specs=[
                 pl.BlockSpec((LEN, wide), lambda i, o: (0, o[0])),
                 pl.BlockSpec((LEN, WIDE), lambda i, o: (0, o[0])),
-                ANY,
+                TOKEN,
             ],
             out_specs=pl.BlockSpec((LEN, wide + WIDE), lambda i, o: (0, 0)),
         ),
@@ -499,8 +499,6 @@
     ]
     *probs_a, done_a = probs_of(jnp.stack([core * 4, core * 2]), queries, keys)
     lines = joined(inner, [done_a])
-    partner = lax.ppermute(for_partner(other[None], queries, keys, lines[0]), "c", swap)
-    *probs_b, done_b = probs_of(jnp.array([0, 2 * PER], jnp.int32), partner, partner)
     turn = (0, -1, 1, 2)
 
     def places(steps):
@@ -510,6 +508,8 @@
 
     held = pltpu.with_memory_space_constraint(normed, pltpu.HBM)
     some, done_some = project(places((0,)), held, normed_b, lines[:1], lines[1:])
+    partner = lax.ppermute(for_partner(other[None], queries, keys, done_some), "c", swap)
+    *probs_b, done_b = probs_of(jnp.array([0, 2 * PER], jnp.int32), partner, partner)
     (_, *a, a_far, a_far2), (_, *b, b_far, b_far2) = rings(lines, "zx", [done_b, done_some])
     most, _ = project(places((-1, 1)), held, normed_b, a, b, some)
     projected = project(
@@ -527,7 +527,7 @@
     total = jnp.sum(rows, axis=0)
     h_c = lax.ppermute(h, "c", swap)
     h_y = lax.ppermute(h, "yl", swap)
-    h_yc = lax.ppermute(h, ("yl", "c"), [(i, 3 - i) for i in range(4)])
+    h_yc = lax.ppermute(h_y, "c", swap)
 
     def in_order(flag, a, b, axis):
         return jnp.where(

time: 207 us -> 218 us (1.053)
  waiting for transfers between devices: 78.6 us -> 86.7 us
  starting transfers between devices: 43.7 us -> 48.4 us
  Pallas kernels: 67.4 us -> 62.9 us
  local copies, waits for them, and re-layouts: 6.86 us -> 9.05 us
    ppermute x14, waiting for transfers between devices: 13 us -> 20.4 us  [hop(): return lax.ppermute(x, axis, [(i, (i + by) % 4) for i in range(4)])]
    ppermute x1, starting transfers between devices: 1.23 us -> 4.49 us  [body(): h_y = lax.ppermute(h, 'yl', swap)]
    unnamed x30 -> x34, local copies, waits for them, and re-layouts: 6.01 us -> 8.2 us
  transfers between devices with their start and end apart: 22 -> 22, of which waited for: 9 -> 8; matrix products, arithmetic and copies ran while one was open for 1% -> 1% of each run, Pallas kernels for 15% -> 10%
where the time goes in v4:
time: 218 us; the launch traced here: 214 us
  waiting for transfers between devices  86.7 us (40%)
  Pallas kernels  62.9 us (29%)
  starting transfers between devices  48.4 us (22%)
  local copies, waits for them, and re-layouts  9.05 us (4%)
  between operations  5.6 us (3%)
    all_to_all x1, waiting for transfers between devices, body(): parts = lax.all_to_all(parts, CHIPS, 0, 0, tiled=True)  47.8 us
    ppermute x14, starting transfers between devices, hop(): return lax.ppermute(x, axis, [(i, (i + by) % 4) for i in range(4)])  23.1 us
    pallas_call x3, Pallas kernels, project(): pl.pallas_call(kernel, grid_spec=pltpu.PrefetchScalarGridSpec(num_scalar_...  21.4 us
    ppermute x14, waiting for transfers between devices, hop(): return lax.ppermute(x, axis, [(i, (i + by) % 4) for i in range(4)])  20.4 us
    pallas_call x2, Pallas kernels, probs_of(): pl.pallas_call(_probs_kernel, grid_spec=pltpu.PrefetchScalarGridSpec(num_...  13.5 us
    all_to_all x1, starting transfers between devices, body(): rows = lax.all_to_all(rows, everyone, 0, 0, tiled=True)  11.4 us
    pallas_call x1, Pallas kernels, pull_back(): pl.pallas_call(_pull_kernel, grid=(2, 2, steps), in_specs=[pl.BlockSpec((...  10.4 us
    pallas_call x1, Pallas kernels, curvature(): pl.pallas_call(_ggn_kernel, grid=(depth // G_COLS,), in_specs=[pl.BlockSp...  8.79 us
  transfers between devices with their start and end apart: 22, of which 8 were waited for; matrix products, arithmetic and copies ran while one was open for 1% of the time, Pallas kernels for 10%

profile of v4, /device:TPU:16, one launch (start us, length us, event | category | flops | bytes accessed | tf_op | source)
XLA Modules:
  0.0 214.3 jit_solution(17176511452354172729)
XLA Ops:
  3.3 8.2 %collective-permute-done.1.swapped_ref = bf16[256,512]{1,0:T(8,128)(2,1)S(1)} collective-permute-done((bf16[256,512]{1,0:T(8,128)(2,1)S(1)}, bf16[256,512]{1,0:T(8,128)(2,1)S(1)}, u32[]{:S(2)}, u32[]{:S(2)}) %collective-permute-start.1) | collective-permute-done | bytes 262176 | tf_op jit(solution)/shard_map/ppermute | solution.py:495
  11.5 2.7 %collective-permute-done._.refs_5_.refs_6_.refs_7_.refs_8_.xb_ref = bf16[512,8192]{1,0:T(8,128)(2,1)} collective-permute-done((bf16[512,8192]{1,0:T(8,128)(2,1)}, bf16[512,8192]{1,0:T(8,128)(2,1)}, u32[]{:S(2)}, u32[]{:S(2)}) %collective-permute-start) | collective-permute-done | bytes 8388640 | tf_op jit(solution)/shard_map/ppermute | solution.py:494
  14.3 3.1 %collective-permute-start.4 = (bf16[256,512]{1,0:T(8,128)(2,1)S(1)}, bf16[256,512]{1,0:T(8,128)(2,1)S(1)}, u32[]{:S(2)}, u32[]{:S(2)}) collective-permute-start(bf16[256,512]{1,0:T(8,128)(2,1)S(1)} %get-tuple-element.24.refs_0_), channel_id=1, source_target_pairs={{0,16},{8,24},{16,0},{24,8},{1,17},{9,25},{17,1},{25,9},{2,18},{10... | collective-permute-start | bytes 786440 | tf_op jit(solution)/shard_map/ppermute | solution.py:421
  19.4 3.9 %collective-permute-start.7 = (bf16[256,512]{1,0:T(8,128)(2,1)S(1)}, bf16[256,512]{1,0:T(8,128)(2,1)S(1)}, u32[]{:S(2)}, u32[]{:S(2)}) collective-permute-start(bf16[256,512]{1,0:T(8,128)(2,1)S(1)} %get-tuple-element.25.refs_4_), channel_id=1, source_target_pairs={{0,4},{2,6},{4,0},{6,2},{1,5},{3,7},{5,1},{7,3},{8,12},{10,14},{12... | collective-permute-start | bytes 786440 | tf_op jit(solution)/shard_map/ppermute | solution.py:421
  29.3 6.7 %shard_map.112 = (bf16[256,4096]{1,0:T(8,128)(2,1)}, bf16[512,4096]{1,0:T(8,128)(2,1)}, s32[1]{0:T(128)}) custom-call(s32[2]{0:T(128)S(1)} %pad_add_fusion.1.off, bf16[512,4096]{1,0:T(8,128)(2,1)S(1)} %copy-done.4, bf16[512,512]{1,0:T(8,128)(2,1)S(1)} %copy-done.12), custom_call_target="tpu_custom_call" | custom-call | flops 805306368 | bytes 8388608 | tf_op jit(solution)/shard_map/pallas_call | solution.py:78
  36.8 6.7 %shard_map.116 = (f32[1024,512]{1,0:T(8,128)}, s32[1]{0:T(128)}) custom-call(s32[8]{0:T(128)S(1)} %stack.137.refs_0_, bf16[512,8192]{1,0:T(8,128)(2,1)} %xa_ref.1, bf16[512,8192]{1,0:T(8,128)(2,1)} %xa_ref.1, bf16[512,8192]{1,0:T(8,128)(2,1)} %xa_ref.1, bf16[512,8192]{1,0:T(8,128)(2,1)} %xa_ref.1, ...), custom_call_target="tpu_custom_call" | custom-call | flops 2147483648 | bytes 6291456 | tf_op jit(solution)/shard_map/pallas_call | solution.py:176
  44.3 2.2 %collective-permute-start.10 = (bf16[1024,512]{1,0:T(8,128)(2,1)S(1)}, bf16[1024,512]{1,0:T(8,128)(2,1)S(1)}, u32[]{:S(2)}, u32[]{:S(2)}) collective-permute-start(bf16[1024,512]{1,0:T(8,128)(2,1)S(1)} %get-tuple-element.27.refs_9_), channel_id=1, source_target_pairs={{0,6},{2,0},{4,2},{6,4},{1,7},{3,1},{5,3},{7,5},{8,14},{10,8},{12,... | collective-permute-start | bytes 3145736 | tf_op jit(solution)/shard_map/ppermute | solution.py:421
  46.5 2.8 %collective-permute-start.12 = (bf16[1024,512]{1,0:T(8,128)(2,1)S(1)}, bf16[1024,512]{1,0:T(8,128)(2,1)S(1)}, u32[]{:S(2)}, u32[]{:S(2)}) collective-permute-start(bf16[1024,512]{1,0:T(8,128)(2,1)S(1)} %get-tuple-element.28.refs_10_), channel_id=1, source_target_pairs={{0,24},{8,0},{16,8},{24,16},{1,25},{9,1},{17,9},{25,17},{2,26},{10... | collective-permute-start | bytes 3145736 | tf_op jit(solution)/shard_map/ppermute | solution.py:421
  49.3 6.8 %shard_map.118 = (bf16[256,4096]{1,0:T(8,128)(2,1)}, bf16[512,4096]{1,0:T(8,128)(2,1)}, s32[1]{0:T(128)}) custom-call(s32[2]{0:T(128)S(1)} %iota_multiply_fusion.off, bf16[512,2304]{1,0:T(8,128)(2,1)S(1)} %collective-permute-done.8.q_ref.k_ref, bf16[512,2304]{1,0:T(8,128)(2,1)S(1)} %collective-permute-done.8.q_ref.k_ref), custom_call_target="tpu_custom_call" | custom-call | flops 805306368 | bytes 8388608 | tf_op jit(solution)/shard_map/pallas_call | solution.py:78
  56.1 13.9 %collective-permute-done.10.refs_1_.refs_10_ = bf16[1024,512]{1,0:T(8,128)(2,1)S(1)} collective-permute-done((bf16[1024,512]{1,0:T(8,128)(2,1)S(1)}, bf16[1024,512]{1,0:T(8,128)(2,1)S(1)}, u32[]{:S(2)}, u32[]{:S(2)}) %collective-permute-start.10) | collective-permute-done | bytes 1048608 | tf_op jit(solution)/shard_map/ppermute | solution.py:421
  70.0 2.9 %collective-permute-done.9.refs_0_.refs_9_ = bf16[1024,512]{1,0:T(8,128)(2,1)S(1)} collective-permute-done((bf16[1024,512]{1,0:T(8,128)(2,1)S(1)}, bf16[1024,512]{1,0:T(8,128)(2,1)S(1)}, u32[]{:S(2)}, u32[]{:S(2)}) %collective-permute-start.9) | collective-permute-done | bytes 1048608 | tf_op jit(solution)/shard_map/ppermute | solution.py:421
  73.0 2.5 %collective-permute-done.11.refs_2_.refs_11_ = bf16[1024,512]{1,0:T(8,128)(2,1)S(1)} collective-permute-done((bf16[1024,512]{1,0:T(8,128)(2,1)S(1)}, bf16[1024,512]{1,0:T(8,128)(2,1)S(1)}, u32[]{:S(2)}, u32[]{:S(2)}) %collective-permute-start.11) | collective-permute-done | bytes 1048608 | tf_op jit(solution)/shard_map/ppermute | solution.py:421
  75.5 2.7 %shard_map.119 = (bf16[512,512]{1,0:T(8,128)(2,1)}, bf16[512,512]{1,0:T(8,128)(2,1)}, bf16[512,512]{1,0:T(8,128)(2,1)}, bf16[512,512]{1,0:T(8,128)(2,1)}) custom-call(bf16[1024,512]{1,0:T(8,128)(2,1)S(1)} %collective-permute-done.9.refs_0_.refs_9_, bf16[1024,512]{1,0:T(8,128)(2,1)S(1)} %collective-permute-done.10.refs_1_.refs_10_, ...), custom_call_target="tpu_custom_call" | custom-call | tf_op jit(solution)/shard_map/pallas_call | solution.py:358
  82.4 3.2 %collective-permute-start.16 = (bf16[512,512]{1,0:T(8,128)(2,1)}, bf16[512,512]{1,0:T(8,128)(2,1)}, u32[]{:S(2)}, u32[]{:S(2)}) collective-permute-start(bf16[512,512]{1,0:T(8,128)(2,1)} %get-tuple-element.36), channel_id=1, source_target_pairs={{0,24},{8,0},{16,8},{24,16},{1,25},{9,1},{17,9},{25,17},{2,26},{10... | collective-permute-start | bytes 1572872 | tf_op jit(solution)/shard_map/ppermute | solution.py:421
  88.6 8.4 %shard_map.120 = (f32[1024,512]{1,0:T(8,128)S(1)}, s32[1]{0:T(128)}) custom-call(s32[16]{0:T(128)S(1)} %stack.163.refs_0_, bf16[512,8192]{1,0:T(8,128)(2,1)} %xa_ref.1, bf16[512,8192]{1,0:T(8,128)(2,1)} %xa_ref.1, bf16[512,8192]{1,0:T(8,128)(2,1)} %xa_ref.1, bf16[512,8192]{1,0:T(8,128)(2,1)} %xa_ref.1, ...), custom_call_target="tpu_custom_call" | custom-call | flops 4294967296 | bytes 12582912 | tf_op jit(solution)/shard_map/pallas_call | solution.py:176
  97.1 6.3 %shard_map.121.v_ref.t_ref = bf16[512,1024]{1,0:T(8,128)(2,1)S(1)} custom-call(s32[8]{0:T(128)S(1)} %stack.146.refs_0_, bf16[512,8192]{1,0:T(8,128)(2,1)} %xa_ref.1, bf16[512,8192]{1,0:T(8,128)(2,1)} %xa_ref.1, bf16[512,8192]{1,0:T(8,128)(2,1)} %xa_ref.1, bf16[512,8192]{1,0:T(8,128)(2,1)} %xa_ref.1, ...), custom_call_target="tpu_custom_call" | custom-call | flops 2147483648 | bytes 6291456 | tf_op jit(solution)/shard_map/pallas_call | solution.py:176
  103.6 10.4 %shard_map.122.pa_ref.pb_ref = bf16[256,1024]{1,0:T(8,128)(2,1)S(1)} custom-call(bf16[256,4096]{1,0:T(8,128)(2,1)S(1)} %copy-done.10, bf16[512,4096]{1,0:T(8,128)(2,1)S(1)} %copy-done.6, bf16[256,4096]{1,0:T(8,128)(2,1)S(1)} %copy-done.11, bf16[512,4096]{1,0:T(8,128)(2,1)S(1)} %copy-done.7, bf16[512,1024]{1,0:T(8,128)(2,1)S(1)} %shard_map.121.v_ref.t_ref, ...), custom_call_target="tpu_custom_call" | custom-call | tf_op jit(solution)/shard_map/pallas_call | solution.py:255
  114.1 8.8 %shard_map.123 = bf16[64,256,128]{2,1,0:T(8,128)(2,1)} custom-call(bf16[256,1024]{1,0:T(8,128)(2,1)S(1)} %shard_map.122.pa_ref.pb_ref, bf16[256,1024]{1,0:T(8,128)(2,1)S(1)} %shard_map.122.pa_ref.pb_ref, bf16[512,8192]{1,0:T(8,128)(2,1)S(1)} %bitcast.46, bf16[512,8192]{1,0:T(8,128)(2,1)} %collective-permute-done._.refs_5_.refs_6_.refs_7_.refs_8_.xb_ref), custom_call_target="tpu_custom_call" | custom-call | tf_op jit(solution)/shard_map/pallas_call | solution.py:286
  122.9 8.3 %all-to-all-start = ((bf16[64,256,128]{2,1,0:T(8,128)(2,1)}), bf16[64,256,128]{2,1,0:T(8,128)(2,1)}, u32[]{:S(2)}, u32[]{:S(2)}) async-start(bf16[64,256,128]{2,1,0:T(8,128)(2,1)} %shard_map.123), calls=%async_computation | async-start | bytes 8388608 | tf_op jit(solution)/shard_map/all_to_all | solution.py:520
  132.0 47.8 %all-to-all-done.parts_ref = bf16[64,256,128]{2,1,0:T(8,128)(2,1)} async-done(((bf16[64,256,128]{2,1,0:T(8,128)(2,1)}), bf16[64,256,128]{2,1,0:T(8,128)(2,1)}, u32[]{:S(2)}, u32[]{:S(2)}) %all-to-all-start) | async-done | bytes 4194336 | tf_op jit(solution)/shard_map/all_to_all | solution.py:520
  179.8 4.6 %shard_map.124 = (f32[128,256]{1,0:T(8,128)S(1)}, f32[128,128]{1,0:T(8,128)}) custom-call(s32[2]{0:T(128)S(1)} %pad_add_fusion.at_ref, f32[1]{0:T(128)S(6)} %copy.13.damping_ref, bf16[64,256,128]{2,1,0:T(8,128)(2,1)} %all-to-all-done.parts_ref, f32[256,512]{1,0:T(8,128)S(1)} %copy-done.1, f32[256,512]{1,0:T(8,128)S(1)} %copy-done.9), custom_call_target="tpu_custom_call" | custom-call | tf_op jit(solution)/shard_map/pallas_call | solution.py:459
  184.3 4.5 %collective-permute-start.18 = (f32[128,256]{1,0:T(8,128)S(1)}, f32[128,256]{1,0:T(8,128)S(1)}, u32[]{:S(2)}, u32[]{:S(2)}) collective-permute-start(f32[128,256]{1,0:T(8,128)S(1)} %get-tuple-element.40), channel_id=1, source_target_pairs={{0,64},{64,0},{1,65},{65,1},{2,66},{66,2},{3,67},{67,3},{4,68},{68... | collective-permute-start | bytes 393224 | tf_op jit(solution)/shard_map/ppermute | solution.py:529
  188.8 11.4 %all-to-all-start.1 = ((f32[128,1,128]{2,1,0:T(1,128)}), f32[128,1,128]{2,1,0:T(1,128)S(1)}, u32[]{:S(2)}, u32[]{:S(2)}) async-start(f32[128,1,128]{2,1,0:T(1,128)} %bitcast.39), calls=%async_computation.1 | async-start | bytes 131072 | tf_op jit(solution)/shard_map/all_to_all | solution.py:526
  200.5 7.7 %all-to-all-done.1 = f32[128,1,128]{2,1,0:T(1,128)S(1)} async-done(((f32[128,1,128]{2,1,0:T(1,128)}), f32[128,1,128]{2,1,0:T(1,128)S(1)}, u32[]{:S(2)}, u32[]{:S(2)}) %all-to-all-start.1) | async-done | bytes 65568 | tf_op jit(solution)/shard_map/all_to_all | solution.py:526
  (79 shorter events, 22.3 us)
Async XLA Ops:
  0.6 13.6 %collective-permute-start = (bf16[512,8192]{1,0:T(8,128)(2,1)}, bf16[512,8192]{1,0:T(8,128)(2,1)}, u32[]{:S(2)}, u32[]{:S(2)}) collective-permute-start(bf16[512,8192]{1,0:T(8,128)(2,1)} %xa_ref.1), channel_id=1, source_target_pairs={{0,32},{32,0},{1,33},{33,1},{2,34},{34,2},{3,35},{35,3},{4,36},{36... | collective-permute-start | bytes 25165832 | tf_op jit(solution)/shard_map/ppermute | solution.py:494
  2.8 8.8 %collective-permute-start.1 = (bf16[256,512]{1,0:T(8,128)(2,1)S(1)}, bf16[256,512]{1,0:T(8,128)(2,1)S(1)}, u32[]{:S(2)}, u32[]{:S(2)}) collective-permute-start(bf16[256,512]{1,0:T(8,128)(2,1)S(1)} %shard_map.113.own_ref), channel_id=1, source_target_pairs={{0,65},{65,0},{64,1},{1,64},{2,67},{67,2},{66,3},{3,66},{4,69},{69... | collective-permute-start | bytes 786440 | tf_op jit(solution)/shard_map/ppermute | solution.py:495
  14.3 10.7 %collective-permute-start.4 = (bf16[256,512]{1,0:T(8,128)(2,1)S(1)}, bf16[256,512]{1,0:T(8,128)(2,1)S(1)}, u32[]{:S(2)}, u32[]{:S(2)}) collective-permute-start(bf16[256,512]{1,0:T(8,128)(2,1)S(1)} %get-tuple-element.24.refs_0_), channel_id=1, source_target_pairs={{0,16},{8,24},{16,0},{24,8},{1,17},{9,25},{17,1},{25,9},{2,18},{10... | collective-permute-start | bytes 786440 | tf_op jit(solution)/shard_map/ppermute | solution.py:421
  17.4 18.6 %collective-permute-start.3 = (bf16[256,512]{1,0:T(8,128)(2,1)S(1)}, bf16[256,512]{1,0:T(8,128)(2,1)S(1)}, u32[]{:S(2)}, u32[]{:S(2)}) collective-permute-start(bf16[256,512]{1,0:T(8,128)(2,1)S(1)} %get-tuple-element.24.refs_0_), channel_id=1, source_target_pairs={{0,24},{8,0},{16,8},{24,16},{1,25},{9,1},{17,9},{25,17},{2,26},{10... | collective-permute-start | bytes 786440 | tf_op jit(solution)/shard_map/ppermute | solution.py:421
  18.5 17.5 %collective-permute-start.2 = (bf16[256,512]{1,0:T(8,128)(2,1)S(1)}, bf16[256,512]{1,0:T(8,128)(2,1)S(1)}, u32[]{:S(2)}, u32[]{:S(2)}) collective-permute-start(bf16[256,512]{1,0:T(8,128)(2,1)S(1)} %get-tuple-element.24.refs_0_), channel_id=1, source_target_pairs={{0,8},{8,16},{16,24},{24,0},{1,9},{9,17},{17,25},{25,1},{2,10},{10... | collective-permute-start | bytes 786440 | tf_op jit(solution)/shard_map/ppermute | solution.py:421
  19.4 16.6 %collective-permute-start.7 = (bf16[256,512]{1,0:T(8,128)(2,1)S(1)}, bf16[256,512]{1,0:T(8,128)(2,1)S(1)}, u32[]{:S(2)}, u32[]{:S(2)}) collective-permute-start(bf16[256,512]{1,0:T(8,128)(2,1)S(1)} %get-tuple-element.25.refs_4_), channel_id=1, source_target_pairs={{0,4},{2,6},{4,0},{6,2},{1,5},{3,7},{5,1},{7,3},{8,12},{10,14},{12... | collective-permute-start | bytes 786440 | tf_op jit(solution)/shard_map/ppermute | solution.py:421
  23.3 12.8 %collective-permute-start.6 = (bf16[256,512]{1,0:T(8,128)(2,1)S(1)}, bf16[256,512]{1,0:T(8,128)(2,1)S(1)}, u32[]{:S(2)}, u32[]{:S(2)}) collective-permute-start(bf16[256,512]{1,0:T(8,128)(2,1)S(1)} %get-tuple-element.25.refs_4_), channel_id=1, source_target_pairs={{0,6},{2,0},{4,2},{6,4},{1,7},{3,1},{5,3},{7,5},{8,14},{10,8},{12,... | collective-permute-start | bytes 786440 | tf_op jit(solution)/shard_map/ppermute | solution.py:421
  25.0 11.0 %collective-permute-start.5 = (bf16[256,512]{1,0:T(8,128)(2,1)S(1)}, bf16[256,512]{1,0:T(8,128)(2,1)S(1)}, u32[]{:S(2)}, u32[]{:S(2)}) collective-permute-start(bf16[256,512]{1,0:T(8,128)(2,1)S(1)} %get-tuple-element.25.refs_4_), channel_id=1, source_target_pairs={{0,2},{2,4},{4,6},{6,0},{1,3},{3,5},{5,7},{7,1},{8,10},{10,12},{12... | collective-permute-start | bytes 786440 | tf_op jit(solution)/shard_map/ppermute | solution.py:421
  44.2 5.1 %collective-permute-start.8 = (bf16[512,2304]{1,0:T(8,128)(2,1)S(1)}, bf16[512,2304]{1,0:T(8,128)(2,1)S(1)}, u32[]{:S(2)}, u32[]{:S(2)}) collective-permute-start(bf16[512,2304]{1,0:T(8,128)(2,1)S(1)} %shard_map.117), channel_id=1, source_target_pairs={{0,32},{32,0},{1,33},{33,1},{2,34},{34,2},{3,35},{35,3},{4,36},{36... | collective-permute-start | bytes 7077896 | tf_op jit(solution)/shard_map/ppermute | solution.py:511
  44.3 25.7 %collective-permute-start.10 = (bf16[1024,512]{1,0:T(8,128)(2,1)S(1)}, bf16[1024,512]{1,0:T(8,128)(2,1)S(1)}, u32[]{:S(2)}, u32[]{:S(2)}) collective-permute-start(bf16[1024,512]{1,0:T(8,128)(2,1)S(1)} %get-tuple-element.27.refs_9_), channel_id=1, source_target_pairs={{0,6},{2,0},{4,2},{6,4},{1,7},{3,1},{5,3},{7,5},{8,14},{10,8},{12,... | collective-permute-start | bytes 3145736 | tf_op jit(solution)/shard_map/ppermute | solution.py:421
  46.5 26.4 %collective-permute-start.9 = (bf16[1024,512]{1,0:T(8,128)(2,1)S(1)}, bf16[1024,512]{1,0:T(8,128)(2,1)S(1)}, u32[]{:S(2)}, u32[]{:S(2)}) collective-permute-start(bf16[1024,512]{1,0:T(8,128)(2,1)S(1)} %get-tuple-element.27.refs_9_), channel_id=1, source_target_pairs={{0,2},{2,4},{4,6},{6,0},{1,3},{3,5},{5,7},{7,1},{8,10},{10,12},{12... | collective-permute-start | bytes 3145736 | tf_op jit(solution)/shard_map/ppermute | solution.py:421
  46.5 26.4 %collective-permute-start.12 = (bf16[1024,512]{1,0:T(8,128)(2,1)S(1)}, bf16[1024,512]{1,0:T(8,128)(2,1)S(1)}, u32[]{:S(2)}, u32[]{:S(2)}) collective-permute-start(bf16[1024,512]{1,0:T(8,128)(2,1)S(1)} %get-tuple-element.28.refs_10_), channel_id=1, source_target_pairs={{0,24},{8,0},{16,8},{24,16},{1,25},{9,1},{17,9},{25,17},{2,26},{10... | collective-permute-start | bytes 3145736 | tf_op jit(solution)/shard_map/ppermute | solution.py:421
  49.3 26.2 %collective-permute-start.11 = (bf16[1024,512]{1,0:T(8,128)(2,1)S(1)}, bf16[1024,512]{1,0:T(8,128)(2,1)S(1)}, u32[]{:S(2)}, u32[]{:S(2)}) collective-permute-start(bf16[1024,512]{1,0:T(8,128)(2,1)S(1)} %get-tuple-element.28.refs_10_), channel_id=1, source_target_pairs={{0,8},{8,16},{16,24},{24,0},{1,9},{9,17},{17,25},{25,1},{2,10},{10... | collective-permute-start | bytes 3145736 | tf_op jit(solution)/shard_map/ppermute | solution.py:421
  79.1 17.9 %collective-permute-start.13 = (bf16[512,512]{1,0:T(8,128)(2,1)}, bf16[512,512]{1,0:T(8,128)(2,1)}, u32[]{:S(2)}, u32[]{:S(2)}) collective-permute-start(bf16[512,512]{1,0:T(8,128)(2,1)} %get-tuple-element.33), channel_id=1, source_target_pairs={{0,2},{2,4},{4,6},{6,0},{1,3},{3,5},{5,7},{7,1},{8,10},{10,12},{12... | collective-permute-start | bytes 1572872 | tf_op jit(solution)/shard_map/ppermute | solution.py:421
  80.7 16.3 %collective-permute-start.14 = (bf16[512,512]{1,0:T(8,128)(2,1)}, bf16[512,512]{1,0:T(8,128)(2,1)}, u32[]{:S(2)}, u32[]{:S(2)}) collective-permute-start(bf16[512,512]{1,0:T(8,128)(2,1)} %get-tuple-element.34), channel_id=1, source_target_pairs={{0,6},{2,0},{4,2},{6,4},{1,7},{3,1},{5,3},{7,5},{8,14},{10,8},{12,... | collective-permute-start | bytes 1572872 | tf_op jit(solution)/shard_map/ppermute | solution.py:421
  82.4 14.6 %collective-permute-start.15 = (bf16[512,512]{1,0:T(8,128)(2,1)}, bf16[512,512]{1,0:T(8,128)(2,1)}, u32[]{:S(2)}, u32[]{:S(2)}) collective-permute-start(bf16[512,512]{1,0:T(8,128)(2,1)} %get-tuple-element.35), channel_id=1, source_target_pairs={{0,8},{8,16},{16,24},{24,0},{1,9},{9,17},{17,25},{25,1},{2,10},{10... | collective-permute-start | bytes 1572872 | tf_op jit(solution)/shard_map/ppermute | solution.py:421
  82.4 14.6 %collective-permute-start.16 = (bf16[512,512]{1,0:T(8,128)(2,1)}, bf16[512,512]{1,0:T(8,128)(2,1)}, u32[]{:S(2)}, u32[]{:S(2)}) collective-permute-start(bf16[512,512]{1,0:T(8,128)(2,1)} %get-tuple-element.36), channel_id=1, source_target_pairs={{0,24},{8,0},{16,8},{24,16},{1,25},{9,1},{17,9},{25,17},{2,26},{10... | collective-permute-start | bytes 1572872 | tf_op jit(solution)/shard_map/ppermute | solution.py:421
  122.9 56.9 %copy-start.9 = (f32[256,512]{1,0:T(8,128)S(1)}, f32[256,512]{1,0:T(8,128)}, u32[]{:S(2)}) copy-start(f32[256,512]{1,0:T(8,128)} %r_ref.1) | copy-start | bytes 1572868
  122.9 56.9 %all-to-all-start = ((bf16[64,256,128]{2,1,0:T(8,128)(2,1)}), bf16[64,256,128]{2,1,0:T(8,128)(2,1)}, u32[]{:S(2)}, u32[]{:S(2)}) async-start(bf16[64,256,128]{2,1,0:T(8,128)(2,1)} %shard_map.123), calls=%async_computation | async-start | bytes 8388608 | tf_op jit(solution)/shard_map/all_to_all | solution.py:520
  131.2 81.8 %copy-start.14 = (f32[256,512]{1,0:T(8,128)S(1)}, f32[256,512]{1,0:T(8,128)}, u32[]{:S(2)}) copy-start(f32[256,512]{1,0:T(8,128)} %param.13) | copy-start | bytes 1572868
  184.3 24.0 %collective-permute-start.18 = (f32[128,256]{1,0:T(8,128)S(1)}, f32[128,256]{1,0:T(8,128)S(1)}, u32[]{:S(2)}, u32[]{:S(2)}) collective-permute-start(f32[128,256]{1,0:T(8,128)S(1)} %get-tuple-element.40), channel_id=1, source_target_pairs={{0,64},{64,0},{1,65},{65,1},{2,66},{66,2},{3,67},{67,3},{4,68},{68... | collective-permute-start | bytes 393224 | tf_op jit(solution)/shard_map/ppermute | solution.py:529
  188.8 19.3 %all-to-all-start.1 = ((f32[128,1,128]{2,1,0:T(1,128)}), f32[128,1,128]{2,1,0:T(1,128)S(1)}, u32[]{:S(2)}, u32[]{:S(2)}) async-start(f32[128,1,128]{2,1,0:T(1,128)} %bitcast.39), calls=%async_computation.1 | async-start | bytes 131072 | tf_op jit(solution)/shard_map/all_to_all | solution.py:526
  200.2 12.6 %collective-permute-start.17 = (f32[128,256]{1,0:T(8,128)S(1)}, f32[128,256]{1,0:T(8,128)S(1)}, u32[]{:S(2)}, u32[]{:S(2)}) collective-permute-start(f32[128,256]{1,0:T(8,128)S(1)} %get-tuple-element.40), channel_id=1, source_target_pairs={{0,32},{32,0},{1,33},{33,1},{2,34},{34,2},{3,35},{35,3},{4,36},{36... | collective-permute-start | bytes 393224 | tf_op jit(solution)/shard_map/ppermute | solution.py:528
  208.3 4.6 %collective-permute-start.19 = (f32[128,256]{1,0:T(8,128)S(1)}, f32[128,256]{1,0:T(8,128)S(1)}, u32[]{:S(2)}, u32[]{:S(2)}) collective-permute-start(f32[128,256]{1,0:T(8,128)S(1)} %collective-permute-done.18), channel_id=1, source_target_pairs={{0,32},{32,0},{1,33},{33,1},{2,34},{34,2},{3,35},{35,3},{4,36},{36... | collective-permute-start | bytes 393224 | tf_op jit(solution)/shard_map/ppermute | solution.py:530
  (15 other events, 131.3 us)
